TPU v7x, 512 devices: a whole 4x8x8 slice. The times are simulated.
512 devices in a mesh: req: 8 (over y), head: 8 (over z), exp: 8 (over x, core).
Axes of the slice: x: 4, y: 8, z: 8, core: 2. Of those that a mesh axis runs over, the one named last changes fastest.
Arguments:
- query: bfloat16 [2, 512, 3072], P(None, ('req', 'exp'), 'head'), may hold values from -125 to 125
- cache_keys: bfloat16 [2, 512, 32, 1024], P(None, ('req', 'exp'), None, 'head'), may hold values from -5 to 5
- cache_values: bfloat16 [2, 512, 32, 1024], P(None, ('req', 'exp'), None, 'head'), may hold values from -12 to 12
- lengths: int32 [2, 512], P(None, ('req', 'exp')), may hold values from 2 to 32, as said below
- out_proj: bfloat16 [3072, 3072], P('head', 'exp'), may hold values from -0.109375 to 0.109375
- residual: bfloat16 [2, 512, 3072], P(None, ('req', 'head'), 'exp'), may hold values from -3 to 3
- norm_gain: bfloat16 [3072], P('exp'), may hold values from 0.099609375 to 1.8984375
- router: bfloat16 [3072, 8], P('exp'), may hold values from -0.109375 to 0.109375
- expert_ids: int32 [2, 512, 2], P(None, ('req', 'head')), may hold values from 0 to 7, all different within a row; in each aligned block of 8 rows (0 to 7, 8 to 15, ..., all dimensions but the last counted through in order) at most 4 rows name the same one
- gate_weight: bfloat16 [8, 3072, 16384], P('exp', None, ('req', 'head')), may hold values from -0.109375 to 0.109375
- up_weight: bfloat16 [8, 3072, 16384], P('exp', None, ('req', 'head')), may hold values from -0.109375 to 0.109375
- down_weight: bfloat16 [8, 16384, 3072], P('exp', 'req', 'head'), may hold values from -0.046875 to 0.046875
Outputs:
- layer_out: bfloat16 [2, 512, 3072], P(None, ('req', 'head'), 'exp')
Inputs may be any that keep to these rules, and one draw needn't show every extreme that they name: `lengths`: positions at or past a request's length are not read; in every micro-batch some request has all 32 positions valid. `expert_ids`: A token names 2 different experts. Within each aligned block of 8 tokens of a micro-batch (one group), no expert is named more than 4 times, a bound that some block reaches.
All inputs are finite; a program needn't handle non-finite values.
Results may differ from a plain program's by a relative error of at most 0.0068.
Values may be sent and summed in bfloat16 or wider, within the bound.
A program may use at most 64 MiB of HBM per device.

v0:
```python
import jax
import jax.numpy as jnp
from jax import lax
from jax.sharding import PartitionSpec as P

D = 3072
HEAD_DIM = 128
TOP = 2


def attend(query_rows, key_rows, value_rows, lengths_now):
    row_count = query_rows.shape[0]
    positions = key_rows.shape[1]
    key_heads = key_rows.shape[2] // HEAD_DIM
    per_group = query_rows.shape[1] // (key_heads * HEAD_DIM)
    queries = query_rows.reshape(row_count, key_heads, per_group, HEAD_DIM)
    keys_split = key_rows.reshape(row_count, positions, key_heads, HEAD_DIM)
    values_split = value_rows.reshape(row_count, positions, key_heads, HEAD_DIM)
    scores = jnp.einsum(
        "tjgd,tljd->tjgl", queries, keys_split, preferred_element_type=jnp.float32
    ) * HEAD_DIM ** (-0.5)
    allowed = jnp.arange(positions, dtype=jnp.int32)[None, :] < lengths_now[:, None]
    scores = jnp.where(allowed[:, None, None, :], scores, jnp.float32(-1e30))
    highest = jnp.max(scores, axis=-1, keepdims=True)
    exponents = jnp.exp(scores - highest)
    weights_now = (exponents / jnp.sum(exponents, axis=-1, keepdims=True)).astype(jnp.bfloat16)
    mixed_out = jnp.einsum(
        "tjgl,tljd->tjgd", weights_now, values_split, preferred_element_type=jnp.float32
    )
    return mixed_out.reshape(row_count, key_heads * per_group * HEAD_DIM).astype(jnp.bfloat16)


def expert_hidden(row_block, gate_local, up_local):
    gate_act = jnp.dot(row_block, gate_local, preferred_element_type=jnp.float32)
    up_act = jnp.dot(row_block, up_local, preferred_element_type=jnp.float32)
    return (jax.nn.silu(gate_act) * up_act).astype(jnp.bfloat16)


def placement_tables(ids_rows, experts, capacity):
    tokens_now = ids_rows.shape[-2]
    onehot = (ids_rows[..., None] == jnp.arange(experts, dtype=jnp.int32)).astype(jnp.float32)
    member = jnp.sum(onehot, axis=-2)
    lower_mask = (jnp.arange(tokens_now)[:, None] > jnp.arange(tokens_now)[None, :]).astype(
        jnp.float32
    )
    earlier = jnp.einsum("st,...te->...se", lower_mask, member, precision=lax.Precision.HIGHEST)
    slot_index = jnp.sum(onehot * earlier[..., None, :], axis=-1)
    slot_hot = (slot_index[..., None] == jnp.arange(capacity, dtype=jnp.float32)).astype(
        jnp.float32
    )
    return (onehot, onehot[..., :, None] * slot_hot[..., None, :])


def per_device(
    query,
    cache_keys,
    cache_values,
    lengths,
    out_proj,
    residual,
    norm_gain,
    router,
    expert_ids,
    gate_weight,
    up_weight,
    down_weight,
):
    micro_count = query.shape[0]
    group_tokens = query.shape[1]
    experts = router.shape[1]
    capacity = 2 * group_tokens * TOP // experts
    gain_full = norm_gain.astype(jnp.float32)
    router_full = router.astype(jnp.float32)
    gate_local = gate_weight[0]
    up_local = up_weight[0]
    down_local = down_weight[0]
    width_head = down_local.shape[1]
    heads_now = lax.axis_size("head")
    results = []
    for micro_index in range(micro_count):
        attended = attend(
            query[micro_index],
            cache_keys[micro_index],
            cache_values[micro_index],
            lengths[micro_index],
        )
        gathered = lax.all_gather(attended, "exp", axis=0, tiled=True)
        projected = lax.psum_scatter(
            jnp.dot(gathered, out_proj, preferred_element_type=jnp.float32),
            "head",
            scatter_dimension=0,
            tiled=True,
        )
        stream = (residual[micro_index].astype(jnp.float32) + projected).astype(jnp.bfloat16)
        stream_full = stream.astype(jnp.float32)
        squares = jnp.sum(stream_full * stream_full, axis=-1)
        scaled = stream_full * gain_full
        total_squares = lax.psum(squares, "exp")
        inverse = lax.rsqrt(total_squares / D + 1e-05)
        normed_full = scaled * inverse[:, None]
        logits = lax.psum(jnp.dot(normed_full, router_full, precision=lax.Precision.HIGHEST), "exp")
        normed = normed_full.astype(jnp.bfloat16)
        chosen_ids = expert_ids[micro_index]
        onehot, placement = placement_tables(chosen_ids, experts, capacity)
        chosen = jnp.sum(onehot * logits[:, None, :], axis=-1)
        exponents = jnp.exp(chosen)
        mixing = exponents / jnp.sum(exponents, axis=1, keepdims=True)
        dispatch = jnp.sum(placement, axis=1).astype(jnp.bfloat16)
        buffer = jnp.einsum(
            "tec,td->ecd", dispatch, normed, preferred_element_type=jnp.float32
        ).astype(jnp.bfloat16)
        own_rows = lax.all_to_all(buffer, "exp", split_axis=0, concat_axis=2, tiled=True)
        hidden = expert_hidden(
            lax.all_gather(own_rows[0], ("req", "head"), axis=0, tiled=True), gate_local, up_local
        )
        down_part = jnp.dot(
            lax.all_gather(hidden, "head", axis=1, tiled=True),
            down_local,
            preferred_element_type=jnp.float32,
        )
        expert_out = lax.psum_scatter(down_part, "req", scatter_dimension=0, tiled=True).astype(
            jnp.bfloat16
        )
        returned_rows = lax.all_to_all(
            lax.all_to_all(
                expert_out.reshape(heads_now, capacity, width_head),
                "head",
                split_axis=0,
                concat_axis=2,
                tiled=True,
            ),
            "exp",
            split_axis=2,
            concat_axis=0,
            tiled=True,
        )
        picked = jnp.einsum(
            "tkec,ecd->tkd",
            placement.astype(jnp.bfloat16),
            returned_rows,
            preferred_element_type=jnp.float32,
        )
        expert_mix = jnp.sum(mixing[:, :, None] * picked, axis=1)
        results.append((stream_full + expert_mix).astype(jnp.bfloat16))
    return jnp.stack(results)


def solution(mesh):
    in_specs = (
        P(None, ("req", "exp"), "head"),
        P(None, ("req", "exp"), None, "head"),
        P(None, ("req", "exp"), None, "head"),
        P(None, ("req", "exp")),
        P("head", "exp"),
        P(None, ("req", "head"), "exp"),
        P("exp"),
        P("exp", None),
        P(None, ("req", "head"), None),
        P("exp", None, ("req", "head")),
        P("exp", None, ("req", "head")),
        P("exp", "req", "head"),
    )
    out_specs = P(None, ("req", "head"), "exp")
    return jax.shard_map(
        per_device, mesh=mesh, in_specs=in_specs, out_specs=out_specs, check_vma=False
    )
```

profile of v0, /device:TPU:1, one launch (start us, length us, event | category | flops | bytes accessed | tf_op | source)
XLA Modules:
  0.0 572.1 jit_solution(1028768122828422089)
XLA Ops:
  6.6 0.8 slice_bitcast_fusion.5
  7.4 0.7 slice_bitcast_fusion.1
  8.2 1.1 fusion.97
  9.3 1.1 fusion.36
  10.4 19.5 %all_gather.18 = bf16[64,384]{1,0:T(8,128)(2,1)S(1)} all-gather(bf16[8,384]{1,0:T(8,128)(2,1)S(1)} %bitcast.168), channel_id=1, replica_groups=mesh['req'=8,'head'=8,'exp'=8] {'exp'}, dimensions={0}, use_global_device_ids=true | all-gather | bytes 55296 | tf_op jit(solution)/shard_map/all_gather | solution.py:87
  29.9 1.1 fusion.96
  31.0 1.1 fusion.37
  32.1 12.8 %all_gather.21 = bf16[64,384]{1,0:T(8,128)(2,1)S(1)} all-gather(bf16[8,384]{1,0:T(8,128)(2,1)S(1)} %bitcast.169), channel_id=1, replica_groups=mesh['req'=8,'head'=8,'exp'=8] {'exp'}, dimensions={0}, use_global_device_ids=true | all-gather | bytes 55296 | tf_op jit(solution)/shard_map/all_gather | solution.py:87
  44.9 1.8 fusion.106
  46.7 1.8 fusion.107
  48.6 1.3 dynamic-slice
  50.6 70.5 %all-reduce.7.cloned.1.call-done = (f32[64,384]{1,0:T(8,128)}, f32[64,384]{1,0:T(8,128)}) async-done(((f32[64,384]{1,0:T(8,128)}, f32[64,384]{1,0:T(8,128)}), (f32[64,384]{1,0:T(8,128)}, f32[64,384]{1,0:T(8,128)})) %all-reduce.7.cloned.1.call-update) | async-done | bytes 196624
  121.1 0.9 fusion.56
  122.0 17.1 %all-reduce.3 = (f32[8]{0:T(128)S(1)}, f32[8]{0:T(128)S(1)}) all-reduce(f32[8]{0:T(128)S(1)} %get-tuple-element.19, f32[8]{0:T(128)S(1)} %get-tuple-element.15), channel_id=1, replica_groups=mesh['req'=8,'head'=8,'exp'=8] {'exp'}, use_global_device_ids=true, to_apply=%region_17.18 | all-reduce | flops 16 | bytes 128 | tf_op jit(solution)/shard_map/psum | solution.py:98
  139.4 12.6 %all-reduce.2 = (f32[8,8]{1,0:T(8,128)S(1)}, f32[8,8]{1,0:T(8,128)S(1)}) all-reduce(f32[8,8]{1,0:T(8,128)S(1)} %fusion.60, f32[8,8]{1,0:T(8,128)S(1)} %fusion.54), channel_id=1, replica_groups=mesh['req'=8,'head'=8,'exp'=8] {'exp'}, use_global_device_ids=true, to_apply=%region_18.19 | all-reduce | flops 128 | bytes 1024 | tf_op jit(solution)/shard_map/psum | solution.py:101
  152.9 8.4 %all_to_all.102 = bf16[8,4,384]{2,1,0:T(4,128)(2,1)} all-to-all(bf16[8,4,384]{2,1,0:T(4,128)(2,1)S(1)} %copy.39), channel_id=1, replica_groups=mesh['req'=8,'head'=8,'exp'=8] {'exp'}, dimensions={0} | all-to-all | bytes 49152 | tf_op jit(solution)/shard_map/all_to_all | solution.py:112
  162.1 8.4 %all_to_all.103 = bf16[8,4,384]{2,1,0:T(4,128)(2,1)} all-to-all(bf16[8,4,384]{2,1,0:T(4,128)(2,1)S(1)} %copy.44), channel_id=1, replica_groups=mesh['req'=8,'head'=8,'exp'=8] {'exp'}, dimensions={0} | all-to-all | bytes 49152 | tf_op jit(solution)/shard_map/all_to_all | solution.py:112
  170.6 65.9 %all-gather.11.cloned.1.call-done = bf16[64,4,3072]{2,1,0:T(4,128)(2,1)} async-done(((bf16[1,4,3072]{2,1,0:T(4,128)(2,1)}), bf16[64,4,3072]{2,1,0:T(4,128)(2,1)}) %all-gather.11.cloned.1.call-update) | async-done | bytes 1572880 | tf_op jit(solution)/shard_map/all_gather | solution.py:114
  236.5 2.7 reshape.202
  239.3 2.1 fusion.12
  241.4 1.2 fusion.23
  242.7 77.2 %all-gather.13.cloned.1.call-done = bf16[64,4,3072]{2,1,0:T(4,128)(2,1)} async-done(((bf16[1,4,3072]{2,1,0:T(4,128)(2,1)}), bf16[64,4,3072]{2,1,0:T(4,128)(2,1)}) %all-gather.13.cloned.1.call-update) | async-done | bytes 1572880 | tf_op jit(solution)/shard_map/all_gather | solution.py:114
  319.9 2.7 reshape.204
  322.6 2.1 fusion.10
  324.7 1.2 fusion.20
  326.0 35.7 %all-gather.7.cloned.1.call-done = bf16[256,2048]{1,0:T(8,128)(2,1)} async-done(((bf16[256,256]{1,0:T(8,128)(2,1)}), bf16[256,2048]{1,0:T(8,128)(2,1)}) %all-gather.7.cloned.1.call-update) | async-done | bytes 1048592 | tf_op jit(solution)/shard_map/all_gather | solution.py:117
  361.7 2.7 fusion.4
  364.4 41.0 %all-gather.9.cloned.1.call-done = bf16[256,2048]{1,0:T(8,128)(2,1)} async-done(((bf16[256,256]{1,0:T(8,128)(2,1)}), bf16[256,2048]{1,0:T(8,128)(2,1)}) %all-gather.9.cloned.1.call-update) | async-done | bytes 1048592 | tf_op jit(solution)/shard_map/all_gather | solution.py:117
  405.4 2.7 fusion.2
  408.1 37.6 %reduce-scatter.3.cloned.1.call-done = f32[32,384]{1,0:T(8,128)} async-done(((f32[256,384]{1,0:T(8,128)}), f32[32,384]{1,0:T(8,128)}) %reduce-scatter.3.cloned.1.call-update) | async-done | bytes 49168 | tf_op jit(solution)/shard_map/reduce_scatter | solution.py:121
  445.7 0.8 convert_element_type.135
  447.1 7.0 %all-to-all-start.1 = ((bf16[8,4,384]{2,1,0:T(4,128)(2,1)}), bf16[8,4,384]{2,1,0:T(4,128)(2,1)S(1)}, u32[]{:S(2)}, u32[]{:S(2)}) async-start(bf16[8,4,384]{2,1,0:T(4,128)(2,1)} %reshape.194), calls=%async_computation.2 | async-start | bytes 49152 | tf_op jit(solution)/shard_map/all_to_all | solution.py:125
  454.2 32.7 %reduce-scatter.5.cloned.1.call-done = f32[32,384]{1,0:T(8,128)} async-done(((f32[256,384]{1,0:T(8,128)}), f32[32,384]{1,0:T(8,128)}) %reduce-scatter.5.cloned.1.call-update) | async-done | bytes 49168 | tf_op jit(solution)/shard_map/reduce_scatter | solution.py:121
  486.9 0.8 convert_element_type.151
  488.3 7.0 %all-to-all-start.4 = ((bf16[8,4,384]{2,1,0:T(4,128)(2,1)}), bf16[8,4,384]{2,1,0:T(4,128)(2,1)S(1)}, u32[]{:S(2)}, u32[]{:S(2)}) async-start(bf16[8,4,384]{2,1,0:T(4,128)(2,1)} %reshape.198), calls=%async_computation.6 | async-start | bytes 49152 | tf_op jit(solution)/shard_map/all_to_all | solution.py:125
  495.4 1.9 copy.40
  497.8 17.9 %reduce.9 = bf16[3072,4]{1,0:T(8,128)(2,1)} reduce(bf16[3072,1,4]{2,1,0:T(2,128)(2,1)S(1)} %bitcast.160, bf16[]{:T(256)} %broadcast.127), dimensions={1}, to_apply=%bitcast.134.reduce_sub_computation | reduce | bytes 49154
  515.6 3.0 reshape.217
  518.7 10.1 %all-to-all-start.2 = ((bf16[8,2,768]{2,1,0:T(2,128)(2,1)}), bf16[8,2,768]{2,1,0:T(2,128)(2,1)S(1)}, u32[]{:S(2)}, u32[]{:S(2)}) async-start(bf16[8,2,768]{2,1,0:T(2,128)(2,1)} %reshape.217), calls=%async_computation.3 | async-start | bytes 49152 | tf_op jit(solution)/shard_map/all_to_all | solution.py:124
  528.8 1.9 copy.45
  530.7 17.9 %reduce.8 = bf16[3072,4]{1,0:T(8,128)(2,1)} reduce(bf16[3072,1,4]{2,1,0:T(2,128)(2,1)S(1)} %bitcast.161, bf16[]{:T(256)} %broadcast.127), dimensions={1}, to_apply=%bitcast.132.reduce_sub_computation | reduce | bytes 49154
  548.6 3.0 reshape.215
  551.6 4.8 all-to-all-start.5
  556.4 2.0 reshape.218
  558.3 1.3 copy.41
  560.0 1.1 all-to-all-done.5
  561.0 2.0 reshape.216
  563.0 1.3 copy.46
  (67 shorter events, 5.4 us)
Async XLA Ops:
  6.5 355.2 %copy-start = (bf16[1,2048,384]{2,1,0:T(8,128)(2,1)S(1)}, bf16[1,2048,384]{2,1,0:T(8,128)(2,1)}, u32[]{:S(2)}) copy-start(bf16[1,2048,384]{2,1,0:T(8,128)(2,1)} %param.23) | copy-start | bytes 4718596
  6.5 42.0 %copy-start.3 = (bf16[384]{0:T(512)(128)(2,1)S(1)}, bf16[384]{0:T(512)(128)(2,1)}, u32[]{:S(2)}) copy-start(bf16[384]{0:T(512)(128)(2,1)} %param.18) | copy-start | bytes 2308
  6.5 42.0 %copy-start.2 = (s32[2,8,2]{1,2,0:T(2,128)S(1)}, s32[2,8,2]{1,2,0:T(2,128)}, u32[]{:S(2)}) copy-start(s32[2,8,2]{1,2,0:T(2,128)} %param.20) | copy-start | bytes 388
  6.5 114.6 %copy-start.1 = (bf16[2,8,384]{2,1,0:T(8,128)(2,1)S(1)}, bf16[2,8,384]{2,1,0:T(8,128)(2,1)}, u32[]{:S(2)}) copy-start(bf16[2,8,384]{2,1,0:T(8,128)(2,1)} %param.17) | copy-start | bytes 36868
  6.5 132.5 %copy-start.6 = (bf16[384,8]{0,1:T(8,128)(2,1)S(1)}, bf16[384,8]{0,1:T(8,128)(2,1)}, u32[]{:S(2)}) copy-start(bf16[384,8]{0,1:T(8,128)(2,1)} %param.19) | copy-start | bytes 18436
  6.5 114.5 %all-reduce.7.cloned.1.call-start = ((), (), s32[]{:S(2)}) async-start(), calls=%async_computation.14 | async-start | bytes 393216
  48.5 188.0 %all-gather.11.cloned.1.call-start = ((), (), s32[]{:S(2)}) async-start(), calls=%async_computation.12 | async-start | bytes 1597440 | tf_op jit(solution)/shard_map/all_gather | solution.py:114
  161.3 158.6 %all-gather.13.cloned.1.call-start = ((), (), s32[]{:S(2)}) async-start(), calls=%async_computation.13 | async-start | bytes 1597440 | tf_op jit(solution)/shard_map/all_gather | solution.py:114
  170.6 191.1 %all-gather.7.cloned.1.call-start = ((), (), s32[]{:S(2)}) async-start(), calls=%async_computation.8 | async-start | bytes 1179648 | tf_op jit(solution)/shard_map/all_gather | solution.py:117
  239.3 2.1 copy-start.4
  242.6 162.8 %all-gather.9.cloned.1.call-start = ((), (), s32[]{:S(2)}) async-start(), calls=%async_computation.10 | async-start | bytes 1179648 | tf_op jit(solution)/shard_map/all_gather | solution.py:117
  322.6 2.1 copy-start.5
  326.0 119.7 %reduce-scatter.3.cloned.1.call-start = ((), (), s32[]{:S(2)}) async-start(), calls=%async_computation.9 | async-start | bytes 442368 | tf_op jit(solution)/shard_map/reduce_scatter | solution.py:121
  364.4 122.5 %reduce-scatter.5.cloned.1.call-start = ((), (), s32[]{:S(2)}) async-start(), calls=%async_computation.11 | async-start | bytes 442368 | tf_op jit(solution)/shard_map/reduce_scatter | solution.py:121
  447.1 41.2 %all-to-all-start.1 = ((bf16[8,4,384]{2,1,0:T(4,128)(2,1)}), bf16[8,4,384]{2,1,0:T(4,128)(2,1)S(1)}, u32[]{:S(2)}, u32[]{:S(2)}) async-start(bf16[8,4,384]{2,1,0:T(4,128)(2,1)} %reshape.194), calls=%async_computation.2 | async-start | bytes 49152 | tf_op jit(solution)/shard_map/all_to_all | solution.py:125
  488.3 30.3 %all-to-all-start.4 = ((bf16[8,4,384]{2,1,0:T(4,128)(2,1)}), bf16[8,4,384]{2,1,0:T(4,128)(2,1)S(1)}, u32[]{:S(2)}, u32[]{:S(2)}) async-start(bf16[8,4,384]{2,1,0:T(4,128)(2,1)} %reshape.198), calls=%async_computation.6 | async-start | bytes 49152 | tf_op jit(solution)/shard_map/all_to_all | solution.py:125
  518.7 32.9 %all-to-all-start.2 = ((bf16[8,2,768]{2,1,0:T(2,128)(2,1)}), bf16[8,2,768]{2,1,0:T(2,128)(2,1)S(1)}, u32[]{:S(2)}, u32[]{:S(2)}) async-start(bf16[8,2,768]{2,1,0:T(2,128)(2,1)} %reshape.217), calls=%async_computation.3 | async-start | bytes 49152 | tf_op jit(solution)/shard_map/all_to_all | solution.py:124
  551.6 9.5 %all-to-all-start.5 = ((bf16[8,2,768]{2,1,0:T(2,128)(2,1)}), bf16[8,2,768]{2,1,0:T(2,128)(2,1)S(1)}, u32[]{:S(2)}, u32[]{:S(2)}) async-start(bf16[8,2,768]{2,1,0:T(2,128)(2,1)} %reshape.215), calls=%async_computation.7 | async-start | bytes 49152 | tf_op jit(solution)/shard_map/all_to_all | solution.py:124
Sparse Core Ops, SparseCore 0:
  48.6 72.4 all-reduce.6
  161.4 75.0 all-gather.10
  240.0 79.7 all-gather.12
  321.9 39.7 all-gather.6
  363.7 41.6 all-gather.8
  408.3 37.3 reduce-scatter.2
  448.5 38.3 reduce-scatter.4
where the time goes:
time: 573 us; the launch traced here: 572 us
  waiting for transfers between devices  362 us (63%)
  blocking collectives  78.9 us (14%)
  other arithmetic  39.8 us (7%)
  starting transfers between devices  29.3 us (5%)
  local copies, waits for them, and re-layouts  26.6 us (5%)
  matrix products  21.5 us (4%)
  between operations  14.4 us (3%)
    all_gather x2, waiting for transfers between devices, per_device(): lax.all_gather(own_rows[0], ('req', 'head'), axis=0, tiled=True)  143 us
    all_gather x2, waiting for transfers between devices, per_device(): lax.all_gather(hidden, 'head', axis=1, tiled=True)  76.6 us
    unnamed x8, waiting for transfers between devices  70.6 us
    reduce_scatter x2, waiting for transfers between devices, per_device(): lax.psum_scatter(down_part, 'req', scatter_dimension=0, tiled=True)  70.3 us
    unnamed x2, other arithmetic  35.7 us
    all_gather x2, blocking collectives, per_device(): gathered = lax.all_gather(attended, 'exp', axis=0, tiled=True)  32.3 us
    unnamed x24, local copies, waits for them, and re-layouts  17.2 us
    psum x1, blocking collectives, per_device(): total_squares = lax.psum(squares, 'exp')  17.1 us
  transfers between devices with their start and end apart: 11, of which 8 were waited for; matrix products, arithmetic and copies ran while one was open for 13% of the time, Pallas kernels for 0%

commit v1 on v0

v1 whole, which is shorter than its diff:
```python
import functools

import jax
import jax.numpy as jnp
from jax import lax
from jax.experimental import pallas as pl
from jax.experimental.pallas import tpu as pltpu
from jax.sharding import PartitionSpec as P

MESH = pl.DeviceIdType.MESH
HEAD_DIM = 128
SLOTS = 4
F32 = jnp.float32
BF16 = jnp.bfloat16
EXACT = lax.Precision.HIGHEST


def iota(shape, axis):
    return lax.broadcasted_iota(jnp.int32, shape, axis)


def dot(a, b, **kw):
    return jnp.dot(a, b, preferred_element_type=F32, **kw)


def dot_t(a, b, **kw):
    return lax.dot_general(a, b, (((1,), (1,)), ((), ())), preferred_element_type=F32, **kw)


class Swap:
    def __init__(self, axis, me, n, src, dst, send_sem, recv_sem):
        self.axis, self.me, self.n, self.src, self.dst = axis, me, n, src, dst
        self.send_sem, self.recv_sem = send_sem, recv_sem

    def copy(self, d, to, at):
        return pltpu.make_async_remote_copy(
            src_ref=self.src(to),
            dst_ref=self.dst(at),
            send_sem=self.send_sem.at[d - 1],
            recv_sem=self.recv_sem.at[d - 1],
            device_id={self.axis: to},
            device_id_type=MESH,
        )

    def start(self):
        for d in range(1, self.n):
            self.copy(d, lax.rem(self.me + d, self.n), self.me).start()

    def wait_recv(self):
        for d in range(1, self.n):
            source = lax.rem(self.me + self.n - d, self.n)
            self.copy(d, source, source).wait_recv()

    def wait_send(self):
        for d in range(1, self.n):
            self.copy(d, lax.rem(self.me + d, self.n), self.me).wait_send()


class Ring:
    def __init__(self, axis, me, n, part, sems):
        self.axis, self.me, self.n, self.part, self.sems = axis, me, n, part, sems
        self.half = n // 2

    def parts(self, way, k):
        if k == self.half:
            return (0,) if way == 0 else (1,)
        return (0, 1)

    def block(self, way, k):
        return lax.rem(self.me + (self.n - k if way == 0 else k), self.n)

    def copy(self, way, k, s):
        to = lax.rem(self.me + (1 if way == 0 else self.n - 1), self.n)
        at = 2 * (k - 1) + (s if k < self.half else 0)
        send_sem, recv_sem = self.sems[2 * way], self.sems[2 * way + 1]
        ref = self.part(self.block(way, k - 1), s)
        return pltpu.make_async_remote_copy(
            src_ref=ref,
            dst_ref=ref,
            send_sem=send_sem.at[at],
            recv_sem=recv_sem.at[at],
            device_id={self.axis: to},
            device_id_type=MESH,
        )

    def arrival(self, way, k, s):
        to = lax.rem(self.me + (1 if way == 0 else self.n - 1), self.n)
        at = 2 * (k - 1) + (s if k < self.half else 0)
        send_sem, recv_sem = self.sems[2 * way], self.sems[2 * way + 1]
        ref = self.part(self.block(way, k), s)
        return pltpu.make_async_remote_copy(
            src_ref=ref,
            dst_ref=ref,
            send_sem=send_sem.at[at],
            recv_sem=recv_sem.at[at],
            device_id={self.axis: to},
            device_id_type=MESH,
        )

    def start(self, s):
        for way in (0, 1):
            if s in self.parts(way, 1):
                self.copy(way, 1, s).start()

    def take(self, way, k, s):
        self.arrival(way, k, s).wait_recv()
        if k < self.half and s in self.parts(way, k + 1):
            self.copy(way, k + 1, s).start()

    def step(self, k):
        for s in (0, 1):
            for way in (0, 1):
                if s in self.parts(way, k):
                    self.take(way, k, s)

    def wait_send(self):
        for k in range(1, self.half + 1):
            for way in (0, 1):
                for s in self.parts(way, k):
                    self.copy(way, k, s).wait_send()


def layer(
    n,
    query_ref,
    keys_hbm,
    values_hbm,
    lengths_ref,
    proj_hbm,
    residual_ref,
    aux_ref,
    ids_ref,
    gate_hbm,
    up_hbm,
    down_hbm,
    out_ref,
    keys,
    values,
    proj,
    wide,
    down,
    aux_all,
    att_all,
    part_own,
    part_send,
    part_recv,
    stream_all,
    first_a,
    first_b,
    rows_a,
    rows_b,
    acc_a,
    acc_b,
    hidden,
    acc,
    down_send,
    down_recv,
    back_send,
    back_recv,
    load_sem,
    aux_sem,
    att_sem,
    part_sem,
    stream_sem,
    first_a_sem,
    first_b_sem,
    ring_a_sem,
    ring_b_sem,
    ring_h_sem,
    down_sem,
    back_sem,
):
    micro, group, width = query_ref.shape
    tokens = micro * group
    slots = micro * SLOTS
    r, h, e = lax.axis_index("req"), lax.axis_index("head"), lax.axis_index("exp")
    features = n * width
    hidden_width = gate_hbm.shape[2]
    positions = keys_hbm.shape[2]

    barrier = pltpu.get_barrier_semaphore()
    for axis, me in (("exp", e), ("head", h), ("req", r)):
        for d in range(1, n):
            pl.semaphore_signal(
                barrier, inc=1, device_id={axis: lax.rem(me + d, n)}, device_id_type=MESH
            )
    for j in range(n):

        @pl.when(jnp.logical_or(h != e, e != j))
        def _():
            pl.semaphore_signal(
                barrier, inc=1, device_id={"head": e, "exp": jnp.int32(j)}, device_id_type=MESH
            )

    loads = [
        pltpu.make_async_copy(keys_hbm, keys, load_sem.at[0]),
        pltpu.make_async_copy(values_hbm, values, load_sem.at[1]),
        pltpu.make_async_copy(proj_hbm, proj, load_sem.at[2]),
        pltpu.make_async_copy(gate_hbm.at[0], wide.at[:, pl.ds(0, hidden_width)], load_sem.at[3]),
        pltpu.make_async_copy(
            up_hbm.at[0], wide.at[:, pl.ds(hidden_width, hidden_width)], load_sem.at[4]
        ),
        pltpu.make_async_copy(down_hbm.at[0], down, load_sem.at[5]),
    ]
    for load in loads:
        load.start()

    per_key = width // HEAD_DIM
    queries = query_ref[...].astype(F32).reshape(tokens, width)
    queries = jnp.concatenate(
        [queries[:, j * HEAD_DIM : (j + 1) * HEAD_DIM] for j in range(per_key)], axis=0
    ).astype(BF16)
    columns = tokens * positions
    owner = iota((1, columns), 1) // positions
    limit = jnp.zeros((1, columns), jnp.int32)
    for t in range(tokens):
        limit = jnp.where(owner == t, lengths_ref[t // group, t % group], limit)
    valid = lax.rem(iota((1, columns), 1), positions) < limit
    owner = jnp.where(valid, owner, -1)
    allowed = lax.rem(iota((per_key * tokens, columns), 0), tokens) == owner
    loads[0].wait()
    scores = dot_t(queries, keys[...].reshape(columns, HEAD_DIM)) * HEAD_DIM ** (-0.5)
    scores = jnp.where(allowed, scores, F32(-1e30))
    exponents = jnp.exp(scores - jnp.max(scores, axis=-1, keepdims=True))
    weights = (exponents / jnp.sum(exponents, axis=-1, keepdims=True)).astype(BF16)
    loads[1].wait()
    mixed = dot(weights, values[...].reshape(columns, HEAD_DIM))
    for j in range(per_key):
        att_all[e, :, j * HEAD_DIM : (j + 1) * HEAD_DIM] = mixed[
            j * tokens : (j + 1) * tokens
        ].astype(BF16)
    aux_all[e] = aux_ref[...]

    pl.semaphore_wait(barrier, 3 * (n - 1) + n - jnp.where(h == e, 1, 0))

    swap_att = Swap("exp", e, n, lambda to: att_all.at[e], lambda at: att_all.at[at], *att_sem)
    swap_aux = Swap("exp", e, n, lambda to: aux_all.at[e], lambda at: aux_all.at[at], *aux_sem)
    swap_att.start()
    swap_aux.start()

    places = n * slots
    ids = [
        jnp.concatenate([ids_ref[m][:, k : k + 1] for m in range(micro)], axis=0) for k in range(2)
    ]
    token_at = iota((tokens, places), 0)
    column = iota((tokens, places), 1)
    hots = [(ids[k] == column // slots).astype(F32) for k in range(2)]
    earlier_of = (
        (iota((tokens, tokens), 1) < iota((tokens, tokens), 0))
        & (iota((tokens, tokens), 1) // group == iota((tokens, tokens), 0) // group)
    ).astype(BF16)
    earlier = dot(earlier_of, (hots[0] + hots[1]).astype(BF16))
    fits = (lax.rem(column, SLOTS).astype(F32) == earlier) & (
        lax.rem(column, slots) // SLOTS == token_at // group
    )
    chosen_at = [jnp.where(fits, hot, F32(0.0)) for hot in hots]
    sel_own = dot_t(
        ((iota((slots, places), 1) - slots * e) == iota((slots, places), 0)).astype(BF16),
        (chosen_at[0] + chosen_at[1]).astype(BF16),
    ).astype(BF16)

    loads[2].wait()
    swap_att.wait_recv()
    partial = dot(att_all[...].reshape(n * tokens, width), proj[...]).reshape(n, tokens, width)
    part_own[...] = partial
    part_send[...] = partial.astype(BF16)
    swap_part = Swap(
        "head", h, n, lambda to: part_send.at[to], lambda at: part_recv.at[at], *part_sem
    )
    swap_part.start()
    projected = part_own[h]
    residual = residual_ref[...].astype(F32).reshape(tokens, width)
    swap_part.wait_recv()
    for d in range(1, n):
        projected += part_recv[lax.rem(h + d, n)].astype(F32)
    stream_all[e] = (residual + projected).astype(BF16)
    swap_stream = Swap(
        "exp", e, n, lambda to: stream_all.at[e], lambda at: stream_all.at[at], *stream_sem
    )
    swap_stream.start()
    swap_aux.wait_recv()
    swap_stream.wait_recv()

    squares = jnp.zeros((tokens, width), F32)
    for j in range(n):
        block = stream_all[j].astype(F32)
        squares += block * block
    inverse = lax.rsqrt(jnp.sum(squares, axis=-1, keepdims=True) / features + 1e-05)
    normed = []
    for j in range(n):
        full = stream_all[j].astype(F32) * aux_all[j].astype(F32)[n : n + 1] * inverse
        normed.append(full)
    quarter = n // 4
    rows = [dot(sel_own, normed[j].astype(BF16)) for j in range(n)]
    for i in range(quarter):
        at = pl.ds(i * width, width)
        first_a[h, :, at] = jnp.concatenate([rows[i], rows[quarter + i]], axis=0).astype(BF16)
        first_b[r, :, at] = jnp.concatenate(
            [rows[2 * quarter + i], rows[3 * quarter + i]], axis=0
        ).astype(BF16)
    swap_a = Swap("head", h, n, lambda to: first_a.at[h], lambda at: first_a.at[at], *first_a_sem)
    swap_b = Swap("req", r, n, lambda to: first_b.at[r], lambda at: first_b.at[at], *first_b_sem)
    swap_a.start()
    swap_b.start()

    logits = jnp.zeros((tokens, 2 * n), F32)
    for j in range(n):
        logits += dot_t(normed[j], aux_all[j].astype(F32), precision=EXACT)
    lane = iota((tokens, 2 * n), 1)
    powers = [
        jnp.exp(jnp.sum(jnp.where(lane == ids[k], logits, F32(0.0)), axis=-1, keepdims=True))
        for k in range(2)
    ]
    total = powers[0] + powers[1]
    mixing = powers[0] / total * chosen_at[0] + powers[1] / total * chosen_at[1]

    half = features // 2
    quarter_width = half // 2

    def settle(first, rows_to, at):
        for i in range(n // 2):
            x, y = first[2 * i].astype(F32), first[2 * i + 1].astype(F32)
            for c in range(2):
                rows_to[
                    at, pl.ds(2 * slots * i, 2 * slots), pl.ds(c * quarter_width, quarter_width)
                ] = jnp.concatenate(
                    [x[c * slots : (c + 1) * slots], y[c * slots : (c + 1) * slots]], axis=0
                ).astype(BF16)

    block_rows = n * slots
    part_rows = block_rows // 2
    ring_a = Ring(
        "req", r, n, lambda b, s: rows_a.at[b, pl.ds(s * part_rows, part_rows)], ring_a_sem
    )
    ring_b = Ring(
        "head", h, n, lambda b, s: rows_b.at[b, pl.ds(s * part_rows, part_rows)], ring_b_sem
    )
    swap_a.wait_recv()
    settle(first_a, rows_a, r)
    ring_a.start(0)
    ring_a.start(1)
    swap_b.wait_recv()
    settle(first_b, rows_b, h)
    ring_b.start(0)
    ring_b.start(1)
    loads[3].wait()
    loads[4].wait()

    def product(rows_from, top, blocks):
        x = [rows_from[b] for b in blocks]
        x = x[0] if len(x) == 1 else jnp.concatenate(x, axis=0)
        return dot(x, wide[pl.ds(top, half), :])

    def multiply(blocks_a, blocks_b):
        y = product(rows_a, 0, blocks_a)
        for i, b in enumerate(blocks_a):
            acc_a[b] = y[i * block_rows : (i + 1) * block_rows]
        y = product(rows_b, half, blocks_b)
        for i, b in enumerate(blocks_b):
            acc_b[b] = y[i * block_rows : (i + 1) * block_rows].reshape(n, slots, 2 * hidden_width)

    multiply([r], [h])
    for k in range(1, n // 2 + 1):
        ring_a.step(k)
        ring_b.step(k)
        ways = (0, 1) if k < n // 2 else (0,)
        multiply([ring_a.block(w, k) for w in ways], [ring_b.block(w, k) for w in ways])

    ring_h = Ring("head", h, n, lambda b, s: hidden.at[b, pl.ds(s * (n // 2), n // 2)], ring_h_sem)

    def activate(b):
        both = acc_a[b] + acc_b[:, b].reshape(block_rows, 2 * hidden_width)
        gated, upward = both[:, :hidden_width], both[:, hidden_width:]
        hidden[h, b] = (gated / (1.0 + jnp.exp(-gated)) * upward).astype(BF16)

    for s in range(2):
        for b in range(s * (n // 2), (s + 1) * (n // 2)):
            activate(b)
        ring_h.start(s)
    loads[5].wait()

    def lower(b, s, first=False):
        at = pl.ds(s * (n // 2), n // 2)
        x = hidden[b, at].reshape(n // 2 * block_rows, hidden_width)
        y = dot(x, down[pl.ds(pl.multiple_of(b * hidden_width, hidden_width), hidden_width), :])
        y = y.reshape(n // 2, block_rows, width)
        acc[at] = y if first else acc[at] + y

    lower(h, 0, True)
    lower(h, 1, True)
    for k in range(1, n // 2 + 1):
        ring_h.step(k)
        for s in range(2):
            for way in (0, 1):
                if s in ring_h.parts(way, k):
                    lower(ring_h.block(way, k), s)

    down_send[...] = acc[...].astype(BF16)
    swap_down = Swap(
        "req", r, n, lambda to: down_send.at[to], lambda at: down_recv.at[at], *down_sem
    )
    swap_down.start()
    expert_rows = acc[r]
    swap_down.wait_recv()
    for d in range(1, n):
        expert_rows += down_recv[lax.rem(r + d, n)].astype(F32)
    back_send[...] = expert_rows.reshape(n, slots, width)

    def back(to, at):
        return pltpu.make_async_remote_copy(
            src_ref=back_send.at[to],
            dst_ref=back_recv.at[at],
            send_sem=back_sem[0].at[to],
            recv_sem=back_sem[1].at[at],
            device_id={"head": jnp.int32(to), "exp": h},
            device_id_type=MESH,
        )

    for j in range(n):

        @pl.when(jnp.logical_or(h != e, h != j))
        def _():
            back(j, e).start()

        @pl.when(jnp.logical_and(h == e, h == j))
        def _():
            back_recv[j] = back_send[j]

    for j in range(n):

        @pl.when(jnp.logical_or(h != e, e != j))
        def _():
            back(j, j).wait_recv()

    returned = back_recv[...].reshape(places, width).astype(BF16).astype(F32)
    result = stream_all[e].astype(F32) + dot(mixing, returned, precision=EXACT)
    out_ref[...] = result.reshape(micro, group, width).astype(BF16)

    for swap in (swap_att, swap_aux, swap_part, swap_stream, swap_a, swap_b, swap_down):
        swap.wait_send()
    for ring in (ring_a, ring_b, ring_h):
        ring.wait_send()
    for j in range(n):

        @pl.when(jnp.logical_or(h != e, h != j))
        def _():
            back(j, e).wait_send()


def per_device(
    n,
    query,
    cache_keys,
    cache_values,
    lengths,
    out_proj,
    residual,
    norm_gain,
    router,
    expert_ids,
    gate_weight,
    up_weight,
    down_weight,
):
    micro, group, width = query.shape
    tokens, slots = micro * group, micro * SLOTS
    features = n * width
    hidden_width = gate_weight.shape[2]
    aux = jnp.concatenate(
        [router.T, norm_gain[None, :], jnp.zeros((n - 1, width), BF16)], axis=0
    )
    vmem = pl.BlockSpec(memory_space=pltpu.VMEM)
    smem = pl.BlockSpec(memory_space=pltpu.SMEM)
    anywhere = pl.BlockSpec(memory_space=pl.ANY)

    def pair(count):
        return (pltpu.SemaphoreType.DMA((count,)), pltpu.SemaphoreType.DMA((count,)))

    ring = (pltpu.SemaphoreType.DMA((n - 1,)),) * 4
    block_rows = n * slots
    scratch = [
        pltpu.VMEM(cache_keys.shape, BF16),
        pltpu.VMEM(cache_values.shape, BF16),
        pltpu.VMEM(out_proj.shape, BF16),
        pltpu.VMEM((features, 2 * hidden_width), BF16),
        pltpu.VMEM(down_weight.shape[1:], BF16),
        pltpu.VMEM((n, 2 * n, width), BF16),
        pltpu.VMEM((n, tokens, width), BF16),
        pltpu.VMEM((n, tokens, width), F32),
        pltpu.VMEM((n, tokens, width), BF16),
        pltpu.VMEM((n, tokens, width), BF16),
        pltpu.VMEM((n, tokens, width), BF16),
        pltpu.VMEM((n, 2 * slots, features // 4), BF16),
        pltpu.VMEM((n, 2 * slots, features // 4), BF16),
        pltpu.VMEM((n, block_rows, features // 2), BF16),
        pltpu.VMEM((n, block_rows, features // 2), BF16),
        pltpu.VMEM((n, block_rows, 2 * hidden_width), F32),
        pltpu.VMEM((n, n, slots, 2 * hidden_width), F32),
        pltpu.VMEM((n, n, block_rows, hidden_width), BF16),
        pltpu.VMEM((n, block_rows, width), F32),
        pltpu.VMEM((n, block_rows, width), BF16),
        pltpu.VMEM((n, block_rows, width), BF16),
        pltpu.VMEM((n, slots, width), F32),
        pltpu.VMEM((n, slots, width), F32),
        pltpu.SemaphoreType.DMA((6,)),
        pair(n - 1),
        pair(n - 1),
        pair(n - 1),
        pair(n - 1),
        pair(n - 1),
        pair(n - 1),
        ring,
        ring,
        ring,
        pair(n - 1),
        pair(n),
    ]
    return pl.pallas_call(
        functools.partial(layer, n),
        out_shape=jax.ShapeDtypeStruct((micro, group, width), BF16),
        in_specs=[
            vmem,
            anywhere,
            anywhere,
            smem,
            anywhere,
            vmem,
            vmem,
            vmem,
            anywhere,
            anywhere,
            anywhere,
        ],
        out_specs=vmem,
        scratch_shapes=scratch,
        compiler_params=pltpu.CompilerParams(
            collective_id=0, has_side_effects=True, vmem_limit_bytes=48 * 1024 * 1024
        ),
    )(
        query,
        cache_keys,
        cache_values,
        lengths,
        out_proj,
        residual,
        aux,
        expert_ids,
        gate_weight,
        up_weight,
        down_weight,
    )


def solution(mesh):
    in_specs = (
        P(None, ("req", "exp"), "head"),
        P(None, ("req", "exp"), None, "head"),
        P(None, ("req", "exp"), None, "head"),
        P(None, ("req", "exp")),
        P("head", "exp"),
        P(None, ("req", "head"), "exp"),
        P("exp"),
        P("exp", None),
        P(None, ("req", "head"), None),
        P("exp", None, ("req", "head")),
        P("exp", None, ("req", "head")),
        P("exp", "req", "head"),
    )
    out_specs = P(None, ("req", "head"), "exp")
    return jax.shard_map(
        functools.partial(per_device, mesh.shape["exp"]),
        mesh=mesh,
        in_specs=in_specs,
        out_specs=out_specs,
        check_vma=False,
    )
```

time: 573 us -> 110 us (0.19)
  waiting for transfers between devices: 362 us -> 0 us
  Pallas kernels: 0 us -> 97.2 us
  blocking collectives: 78.9 us -> 0 us
  other arithmetic: 39.8 us -> 0.76 us
  starting transfers between devices: 29.3 us -> 0 us
  matrix products: 21.5 us -> 0 us
  local copies, waits for them, and re-layouts: 26.6 us -> 11.2 us
  between operations: 14.4 us -> 0.02 us
    all_gather x4 -> x0, waiting for transfers between devices: 220 us -> none  [the longest x2 143 us: per_device(): lax.all_gather(own_rows[0], ('req', 'head'), axis=0, tiled=True)]
    pallas_call x0 -> x1, Pallas kernels: none -> 97.2 us  [per_device(): pl.pallas_call(functools.partial(layer, n), out_shape=jax.ShapeDtypeStruc...]
    unnamed x8 -> x0, waiting for transfers between devices: 70.6 us -> none
    reduce_scatter x2 -> x0, waiting for transfers between devices: 70.3 us -> none  [per_device(): lax.psum_scatter(down_part, 'req', scatter_dimension=0, tiled=True)]
    unnamed x2 -> x0, other arithmetic: 35.7 us -> none
    all_gather x2 -> x0, blocking collectives: 32.3 us -> none  [per_device(): gathered = lax.all_gather(attended, 'exp', axis=0, tiled=True)]
    psum x2 -> x0, blocking collectives: 29.7 us -> none  [the longest x1 17.1 us: per_device(): total_squares = lax.psum(squares, 'exp')]
    all_to_all x4 -> x0, starting transfers between devices: 29 us -> none  [the longest x2 14.9 us: per_device(): lax.all_to_all(lax.all_to_all(expert_out.reshape(heads_now, capacity, wid...]
  transfers between devices with their start and end apart: 11 -> 0, of which waited for: 8 -> 0; matrix products, arithmetic and copies ran while one was open for 13% -> 0% of each run, Pallas kernels for 0% -> 0%
where the time goes in v1:
time: 110 us; the launch traced here: 109 us
  Pallas kernels  97.2 us (88%)
  local copies, waits for them, and re-layouts  11.2 us (10%)
    pallas_call x1, Pallas kernels, per_device(): pl.pallas_call(functools.partial(layer, n), out_shape=jax.ShapeDtypeStruc...  97.2 us
    unnamed x20, local copies, waits for them, and re-layouts  10.4 us

profile of v1, /device:TPU:1, one launch (start us, length us, event | category | flops | bytes accessed | tf_op | source)
XLA Modules:
  0.0 109.2 jit_solution(2925338787796910691)
XLA Ops:
  0.0 0.1 pad.2.clone
  0.1 0.7 broadcast_in_dim.6
  0.8 0.8 copy.13.ids_ref
  1.5 0.8 maximum_maximum_fusion.aux_ref
  2.3 0.0 copy-start
  2.3 1.4 %copy-done = bf16[1,3072,256]{2,1,0:T(8,128)(2,1)S(1)} copy-done((bf16[1,3072,256]{2,1,0:T(8,128)(2,1)S(1)}, bf16[1,3072,256]{2,1,0:T(8,128)(2,1)}, u32[]{:S(2)}) %copy-start) | copy-done | bytes 1572888
  3.7 0.0 copy-start.1
  3.7 1.4 %copy-done.1 = bf16[1,3072,256]{2,1,0:T(8,128)(2,1)S(1)} copy-done((bf16[1,3072,256]{2,1,0:T(8,128)(2,1)S(1)}, bf16[1,3072,256]{2,1,0:T(8,128)(2,1)}, u32[]{:S(2)}) %copy-start.1) | copy-done | bytes 1572888
  5.1 0.0 copy-start.2
  5.1 1.4 %copy-done.2 = bf16[1,2048,384]{2,1,0:T(8,128)(2,1)S(1)} copy-done((bf16[1,2048,384]{2,1,0:T(8,128)(2,1)S(1)}, bf16[1,2048,384]{2,1,0:T(8,128)(2,1)}, u32[]{:S(2)}) %copy-start.2) | copy-done | bytes 1572888
  6.5 0.0 copy-start.3
  6.5 1.0 copy-done.3
  7.5 0.0 copy-start.4
  7.5 0.9 copy-done.4
  8.4 0.0 copy-start.5
  8.4 0.9 copy-done.5
  9.3 0.0 copy-start.6
  9.3 0.7 copy-done.6
  10.0 0.0 copy-start.7
  10.0 0.7 copy-done.7
  10.7 0.0 copy-start.8
  10.7 0.7 copy-done.8
  11.4 97.2 %shard_map.118 = bf16[2,8,384]{2,1,0:T(8,128)(2,1)S(1)} custom-call(bf16[2,8,384]{2,1,0:T(8,128)(2,1)S(1)} %copy-done.6, bf16[2,8,32,128]{3,2,1,0:T(8,128)(2,1)S(1)} %copy-done.4, bf16[2,8,32,128]{3,2,1,0:T(8,128)(2,1)S(1)} %copy-done.5, s32[2,8]{1,0:T(2,128)S(1)} %copy-done.8, bf16[384,384]{1,0:T(8,128)(2,1)S(1)} %copy-done.3, ...), custom_call_target="tpu_custom_call" | custom-call | tf_op jit(solution)/shard_map/pallas_call | solution.py:518
  108.6 0.6 copy.15
  (1 shorter events, 0.0 us)
Async XLA Ops:
  2.3 1.4 %copy-start = (bf16[1,3072,256]{2,1,0:T(8,128)(2,1)S(1)}, bf16[1,3072,256]{2,1,0:T(8,128)(2,1)}, u32[]{:S(2)}) copy-start(bf16[1,3072,256]{2,1,0:T(8,128)(2,1)} %gate_hbm.1) | copy-start | bytes 4718596
  3.7 1.4 %copy-start.1 = (bf16[1,3072,256]{2,1,0:T(8,128)(2,1)S(1)}, bf16[1,3072,256]{2,1,0:T(8,128)(2,1)}, u32[]{:S(2)}) copy-start(bf16[1,3072,256]{2,1,0:T(8,128)(2,1)} %up_hbm.1) | copy-start | bytes 4718596
  5.1 1.4 %copy-start.2 = (bf16[1,2048,384]{2,1,0:T(8,128)(2,1)S(1)}, bf16[1,2048,384]{2,1,0:T(8,128)(2,1)}, u32[]{:S(2)}) copy-start(bf16[1,2048,384]{2,1,0:T(8,128)(2,1)} %down_hbm.1) | copy-start | bytes 4718596
  6.5 1.0 copy-start.3
  7.5 0.9 copy-start.4
  8.4 0.9 copy-start.5
  9.3 0.7 copy-start.6
  10.0 0.7 copy-start.7
  10.7 0.7 copy-start.8

commit v2 on v1

--- a/solution.py
+++ b/solution.py
@@ -128,7 +128,8 @@
     lengths_ref,
     proj_hbm,
     residual_ref,
-    aux_ref,
+    gain_ref,
+    router_ref,
     ids_ref,
     gate_hbm,
     up_hbm,
@@ -229,7 +230,8 @@
         att_all[e, :, j * HEAD_DIM : (j + 1) * HEAD_DIM] = mixed[
             j * tokens : (j + 1) * tokens
         ].astype(BF16)
-    aux_all[e] = aux_ref[...]
+    gain = jnp.broadcast_to(gain_ref[...].astype(F32).reshape(1, width), (n, width))
+    aux_all[e] = jnp.concatenate([router_ref[...].astype(F32), gain], axis=0).astype(BF16)
 
     pl.semaphore_wait(barrier, 3 * (n - 1) + n - jnp.where(h == e, 1, 0))
 
@@ -239,8 +241,16 @@
     swap_aux.start()
 
     places = n * slots
+    diagonal = iota((group, group), 0) == iota((group, group), 1)
+
+    def upright(row):
+        return jnp.sum(jnp.where(diagonal, row, F32(0.0)), axis=-1, keepdims=True)
+
     ids = [
-        jnp.concatenate([ids_ref[m][:, k : k + 1] for m in range(micro)], axis=0) for k in range(2)
+        jnp.concatenate(
+            [upright(ids_ref[m][k : k + 1, :].astype(F32)) for m in range(micro)], axis=0
+        ).astype(jnp.int32)
+        for k in range(2)
     ]
     token_at = iota((tokens, places), 0)
     column = iota((tokens, places), 1)
@@ -466,9 +476,6 @@
     tokens, slots = micro * group, micro * SLOTS
     features = n * width
     hidden_width = gate_weight.shape[2]
-    aux = jnp.concatenate(
-        [router.T, norm_gain[None, :], jnp.zeros((n - 1, width), BF16)], axis=0
-    )
     vmem = pl.BlockSpec(memory_space=pltpu.VMEM)
     smem = pl.BlockSpec(memory_space=pltpu.SMEM)
     anywhere = pl.BlockSpec(memory_space=pl.ANY)
@@ -527,6 +534,7 @@
             vmem,
             vmem,
             vmem,
+            vmem,
             anywhere,
             anywhere,
             anywhere,
@@ -534,7 +542,7 @@
         out_specs=vmem,
         scratch_shapes=scratch,
         compiler_params=pltpu.CompilerParams(
-            collective_id=0, has_side_effects=True, vmem_limit_bytes=48 * 1024 * 1024
+            collective_id=0, has_side_effects=True, vmem_limit_bytes=60 * 1024 * 1024
         ),
     )(
         query,
@@ -543,8 +551,9 @@
         lengths,
         out_proj,
         residual,
-        aux,
-        expert_ids,
+        norm_gain,
+        router.T,
+        expert_ids.transpose(0, 2, 1),
         gate_weight,
         up_weight,
         down_weight,

time: 110 us -> 99.7 us (0.906)
  local copies, waits for them, and re-layouts: 11.2 us -> 1.31 us
    unnamed x20 -> x1, local copies, waits for them, and re-layouts: 10.4 us -> 1.31 us
where the time goes in v2:
time: 99.7 us; the launch traced here: 99.5 us
  Pallas kernels  98.2 us (98%)
  local copies, waits for them, and re-layouts  1.31 us (1%)
    pallas_call x1, Pallas kernels, per_device(): pl.pallas_call(functools.partial(layer, n), out_shape=jax.ShapeDtypeStruc...  98.2 us

profile of v2, /device:TPU:1, one launch (start us, length us, event | category | flops | bytes accessed | tf_op | source)
XLA Modules:
  0.0 99.5 jit_solution(3679893692904444400)
XLA Ops:
  0.0 98.2 %shard_map.118 = bf16[2,8,384]{2,1,0:T(8,128)(2,1)} custom-call(bf16[2,8,384]{2,1,0:T(8,128)(2,1)} %query_ref.1, bf16[2,8,32,128]{3,2,1,0:T(8,128)(2,1)} %keys_hbm.1, bf16[2,8,32,128]{3,2,1,0:T(8,128)(2,1)} %values_hbm.1, s32[2,8]{1,0:T(2,128)} %lengths_ref.1, bf16[384,384]{1,0:T(8,128)(2,1)} %proj_hbm.1, bf16[2,8,384]{2,1,0:T(8,128)(2,1)} %residual_ref.1, ...), custom_call_target="tpu_custom_call" | custom-call | tf_op jit(solution)/shard_map/pallas_call | solution.py:525
  98.2 1.3 %copy.14 = bf16[2,8,384]{2,1,0:T(8,128)(2,1)} copy(bf16[2,8,384]{2,1,0:T(8,128)(2,1)} %shard_map.118) | data formatting | bytes 24576

commit v3 on v2

--- a/solution.py
+++ b/solution.py
@@ -28,16 +28,16 @@
 
 
 class Swap:
-    def __init__(self, axis, me, n, src, dst, send_sem, recv_sem):
+    def __init__(self, axis, me, n, src, dst, sems):
         self.axis, self.me, self.n, self.src, self.dst = axis, me, n, src, dst
-        self.send_sem, self.recv_sem = send_sem, recv_sem
+        self.sems = sems
 
     def copy(self, d, to, at):
         return pltpu.make_async_remote_copy(
             src_ref=self.src(to),
             dst_ref=self.dst(at),
-            send_sem=self.send_sem.at[d - 1],
-            recv_sem=self.recv_sem.at[d - 1],
+            send_sem=self.sems.at[0, d - 1],
+            recv_sem=self.sems.at[1, d - 1],
             device_id={self.axis: to},
             device_id_type=MESH,
         )
@@ -57,67 +57,48 @@
 
 
 class Ring:
-    def __init__(self, axis, me, n, part, sems):
-        self.axis, self.me, self.n, self.part, self.sems = axis, me, n, part, sems
+    def __init__(self, axis, me, n, block_ref, sems):
+        self.axis, self.me, self.n, self.block_ref, self.sems = axis, me, n, block_ref, sems
         self.half = n // 2
-
-    def parts(self, way, k):
-        if k == self.half:
-            return (0,) if way == 0 else (1,)
-        return (0, 1)
 
     def block(self, way, k):
         return lax.rem(self.me + (self.n - k if way == 0 else k), self.n)
 
-    def copy(self, way, k, s):
+    def copy(self, way, k, block):
+        ref = self.block_ref(block)
+        if k == self.half:
+            rows = ref.shape[0] // 2
+            ref = ref.at[pl.ds(way * rows, rows)]
         to = lax.rem(self.me + (1 if way == 0 else self.n - 1), self.n)
-        at = 2 * (k - 1) + (s if k < self.half else 0)
-        send_sem, recv_sem = self.sems[2 * way], self.sems[2 * way + 1]
-        ref = self.part(self.block(way, k - 1), s)
         return pltpu.make_async_remote_copy(
             src_ref=ref,
             dst_ref=ref,
-            send_sem=send_sem.at[at],
-            recv_sem=recv_sem.at[at],
+            send_sem=self.sems.at[2 * way, k - 1],
+            recv_sem=self.sems.at[2 * way + 1, k - 1],
             device_id={self.axis: to},
             device_id_type=MESH,
         )
 
-    def arrival(self, way, k, s):
-        to = lax.rem(self.me + (1 if way == 0 else self.n - 1), self.n)
-        at = 2 * (k - 1) + (s if k < self.half else 0)
-        send_sem, recv_sem = self.sems[2 * way], self.sems[2 * way + 1]
-        ref = self.part(self.block(way, k), s)
-        return pltpu.make_async_remote_copy(
-            src_ref=ref,
-            dst_ref=ref,
-            send_sem=send_sem.at[at],
-            recv_sem=recv_sem.at[at],
-            device_id={self.axis: to},
-            device_id_type=MESH,
-        )
-
-    def start(self, s):
+    def send(self, way, k):
+        self.copy(way, k, self.block(way, k - 1)).start()
+
+    def start(self):
         for way in (0, 1):
-            if s in self.parts(way, 1):
-                self.copy(way, 1, s).start()
-
-    def take(self, way, k, s):
-        self.arrival(way, k, s).wait_recv()
-        if k < self.half and s in self.parts(way, k + 1):
-            self.copy(way, k + 1, s).start()
+            self.send(way, 1)
 
     def step(self, k):
-        for s in (0, 1):
-            for way in (0, 1):
-                if s in self.parts(way, k):
-                    self.take(way, k, s)
+        for way in (0, 1):
+            self.copy(way, k, self.block(way, k)).wait_recv()
+            if k < self.half:
+                self.send(way, k + 1)
+
+    def blocks(self, k):
+        return [self.block(way, k) for way in ((0, 1) if k < self.half else (0,))]
 
     def wait_send(self):
         for k in range(1, self.half + 1):
             for way in (0, 1):
-                for s in self.parts(way, k):
-                    self.copy(way, k, s).wait_send()
+                self.copy(way, k, self.block(way, k - 1)).wait_send()
 
 
 def layer(
@@ -150,8 +131,6 @@
     first_b,
     rows_a,
     rows_b,
-    acc_a,
-    acc_b,
     hidden,
     acc,
     down_send,
@@ -159,16 +138,8 @@
     back_send,
     back_recv,
     load_sem,
-    aux_sem,
-    att_sem,
-    part_sem,
-    stream_sem,
-    first_a_sem,
-    first_b_sem,
-    ring_a_sem,
-    ring_b_sem,
-    ring_h_sem,
-    down_sem,
+    swap_sem,
+    ring_sem,
     back_sem,
 ):
     micro, group, width = query_ref.shape
@@ -235,8 +206,8 @@
 
     pl.semaphore_wait(barrier, 3 * (n - 1) + n - jnp.where(h == e, 1, 0))
 
-    swap_att = Swap("exp", e, n, lambda to: att_all.at[e], lambda at: att_all.at[at], *att_sem)
-    swap_aux = Swap("exp", e, n, lambda to: aux_all.at[e], lambda at: aux_all.at[at], *aux_sem)
+    swap_att = Swap("exp", e, n, lambda to: att_all.at[e], lambda at: att_all.at[at], swap_sem.at[0])
+    swap_aux = Swap("exp", e, n, lambda to: aux_all.at[e], lambda at: aux_all.at[at], swap_sem.at[1])
     swap_att.start()
     swap_aux.start()
 
@@ -275,7 +246,7 @@
     part_own[...] = partial
     part_send[...] = partial.astype(BF16)
     swap_part = Swap(
-        "head", h, n, lambda to: part_send.at[to], lambda at: part_recv.at[at], *part_sem
+        "head", h, n, lambda to: part_send.at[to], lambda at: part_recv.at[at], swap_sem.at[2]
     )
     swap_part.start()
     projected = part_own[h]
@@ -285,7 +256,7 @@
         projected += part_recv[lax.rem(h + d, n)].astype(F32)
     stream_all[e] = (residual + projected).astype(BF16)
     swap_stream = Swap(
-        "exp", e, n, lambda to: stream_all.at[e], lambda at: stream_all.at[at], *stream_sem
+        "exp", e, n, lambda to: stream_all.at[e], lambda at: stream_all.at[at], swap_sem.at[3]
     )
     swap_stream.start()
     swap_aux.wait_recv()
@@ -300,18 +271,91 @@
     for j in range(n):
         full = stream_all[j].astype(F32) * aux_all[j].astype(F32)[n : n + 1] * inverse
         normed.append(full)
-    quarter = n // 4
-    rows = [dot(sel_own, normed[j].astype(BF16)) for j in range(n)]
-    for i in range(quarter):
-        at = pl.ds(i * width, width)
-        first_a[h, :, at] = jnp.concatenate([rows[i], rows[quarter + i]], axis=0).astype(BF16)
-        first_b[r, :, at] = jnp.concatenate(
-            [rows[2 * quarter + i], rows[3 * quarter + i]], axis=0
+    chunks = n // 2
+    packed = chunks * SLOTS
+    stacked = [
+        jnp.concatenate([full.astype(BF16) for full in normed[i * chunks : (i + 1) * chunks]], axis=0)
+        for i in range(2)
+    ]
+    first_swaps = []
+    for m in range(micro):
+        pick = (
+            iota((packed, slots), 1) == m * SLOTS + lax.rem(iota((packed, slots), 0), SLOTS)
         ).astype(BF16)
-    swap_a = Swap("head", h, n, lambda to: first_a.at[h], lambda at: first_a.at[at], *first_a_sem)
-    swap_b = Swap("req", r, n, lambda to: first_b.at[r], lambda at: first_b.at[at], *first_b_sem)
-    swap_a.start()
-    swap_b.start()
+        spread = (
+            lax.rem(iota((tokens, chunks * tokens), 1), tokens)
+            == iota((tokens, chunks * tokens), 0)
+        ).astype(BF16)
+        same = (
+            iota((packed, chunks * tokens), 0) // SLOTS
+            == iota((packed, chunks * tokens), 1) // tokens
+        )
+        take = dot(dot(pick, sel_own).astype(BF16), spread)
+        take = jnp.where(same, take, F32(0.0)).astype(BF16)
+        first_a[m, h] = dot(take, stacked[0]).astype(BF16)
+        first_b[m, r] = dot(take, stacked[1]).astype(BF16)
+        swap_a = Swap(
+            "head",
+            h,
+            n,
+            lambda to, m=m: first_a.at[m, h],
+            lambda at, m=m: first_a.at[m, at],
+            swap_sem.at[4 + 2 * m],
+        )
+        swap_b = Swap(
+            "req",
+            r,
+            n,
+            lambda to, m=m: first_b.at[m, r],
+            lambda at, m=m: first_b.at[m, at],
+            swap_sem.at[5 + 2 * m],
+        )
+        swap_a.start()
+        swap_b.start()
+        first_swaps.append((swap_a, swap_b))
+
+    half = features // 2
+    block_rows = n * SLOTS
+    all_rows = n * block_rows
+    ordered = iota((n * packed, n * packed), 0)
+    ordered = (
+        lax.rem(ordered, block_rows) // SLOTS * packed
+        + ordered // block_rows * SLOTS
+        + lax.rem(ordered, SLOTS)
+        == iota((n * packed, n * packed), 1)
+    ).astype(BF16)
+
+    def settle(first, rows_to):
+        y = dot(ordered, first[...].reshape(n * packed, width)).astype(BF16)
+        for c in range(chunks):
+            rows_to[:, pl.ds(c * width, width)] = y[c * block_rows : (c + 1) * block_rows]
+
+    rings_a = [
+        Ring("req", r, n, lambda b, m=m: rows_a.at[b, m], ring_sem.at[m]) for m in range(micro)
+    ]
+    rings_b = [
+        Ring("head", h, n, lambda b, m=m: rows_b.at[b, m], ring_sem.at[micro + m])
+        for m in range(micro)
+    ]
+    rings_h = [
+        Ring("head", h, n, lambda b, m=m: hidden.at[b, m], ring_sem.at[2 * micro + m])
+        for m in range(micro)
+    ]
+
+    def settle_a(m):
+        first_swaps[m][0].wait_recv()
+        settle(first_a.at[m], rows_a.at[r, m])
+
+    def settle_b(m):
+        first_swaps[m][1].wait_recv()
+        settle(first_b.at[m], rows_b.at[h, m])
+
+    settle_a(0)
+    rings_a[0].start()
+    settle_b(0)
+    rings_b[0].start()
+    settle_a(1)
+    settle_b(1)
 
     logits = jnp.zeros((tokens, 2 * n), F32)
     for j in range(n):
@@ -324,104 +368,105 @@
     total = powers[0] + powers[1]
     mixing = powers[0] / total * chosen_at[0] + powers[1] / total * chosen_at[1]
 
-    half = features // 2
-    quarter_width = half // 2
-
-    def settle(first, rows_to, at):
-        for i in range(n // 2):
-            x, y = first[2 * i].astype(F32), first[2 * i + 1].astype(F32)
-            for c in range(2):
-                rows_to[
-                    at, pl.ds(2 * slots * i, 2 * slots), pl.ds(c * quarter_width, quarter_width)
-                ] = jnp.concatenate(
-                    [x[c * slots : (c + 1) * slots], y[c * slots : (c + 1) * slots]], axis=0
-                ).astype(BF16)
-
-    block_rows = n * slots
-    part_rows = block_rows // 2
-    ring_a = Ring(
-        "req", r, n, lambda b, s: rows_a.at[b, pl.ds(s * part_rows, part_rows)], ring_a_sem
-    )
-    ring_b = Ring(
-        "head", h, n, lambda b, s: rows_b.at[b, pl.ds(s * part_rows, part_rows)], ring_b_sem
-    )
-    swap_a.wait_recv()
-    settle(first_a, rows_a, r)
-    ring_a.start(0)
-    ring_a.start(1)
-    swap_b.wait_recv()
-    settle(first_b, rows_b, h)
-    ring_b.start(0)
-    ring_b.start(1)
+    crossed = iota((all_rows, all_rows), 0)
+    crossed = (
+        lax.rem(crossed, block_rows) // SLOTS * block_rows
+        + crossed // block_rows * SLOTS
+        + lax.rem(crossed, SLOTS)
+        == iota((all_rows, all_rows), 1)
+    ).astype(BF16)
+
+    def activate(m):
+        x = rows_a[:, m].reshape(all_rows, half)
+        y = dot(x, wide[pl.ds(0, half), :])
+        x = dot(crossed, rows_b[:, m].reshape(all_rows, half)).astype(BF16)
+        y += dot(x, wide[pl.ds(half, half), :])
+        gated, upward = y[:, :hidden_width], y[:, hidden_width:]
+        hidden[h, m] = (gated / (1.0 + jnp.exp(-gated)) * upward).astype(BF16)
+        rings_h[m].start()
+
+    def lower(b, m, first=False):
+        y = dot(
+            hidden[b, m], down[pl.ds(pl.multiple_of(b * hidden_width, hidden_width), hidden_width), :]
+        ).reshape(n, block_rows, width)
+        acc[m] = y if first else acc[m] + y
+
+    def gather_step(m, k):
+        rings_a[m].step(k)
+        rings_b[m].step(k)
+
+    def hidden_step(m, k):
+        rings_h[m].step(k)
+        for b in rings_h[m].blocks(k):
+            lower(b, m)
+
+    swaps_down = [
+        Swap(
+            "req",
+            r,
+            n,
+            lambda to, m=m: down_send.at[m, to],
+            lambda at, m=m: down_recv.at[m, at],
+            swap_sem.at[8 + m],
+        )
+        for m in range(micro)
+    ]
+
+    def hand_over(m):
+        down_send[m] = acc[m].astype(BF16)
+        swaps_down[m].start()
+
+    def collect(m):
+        total = acc[m, r]
+        swaps_down[m].wait_recv()
+        for d in range(1, n):
+            total += down_recv[m, lax.rem(r + d, n)].astype(F32)
+        return total.astype(BF16)
+
+    gather_step(0, 1)
+    rings_a[1].start()
+    rings_b[1].start()
     loads[3].wait()
     loads[4].wait()
-
-    def product(rows_from, top, blocks):
-        x = [rows_from[b] for b in blocks]
-        x = x[0] if len(x) == 1 else jnp.concatenate(x, axis=0)
-        return dot(x, wide[pl.ds(top, half), :])
-
-    def multiply(blocks_a, blocks_b):
-        y = product(rows_a, 0, blocks_a)
-        for i, b in enumerate(blocks_a):
-            acc_a[b] = y[i * block_rows : (i + 1) * block_rows]
-        y = product(rows_b, half, blocks_b)
-        for i, b in enumerate(blocks_b):
-            acc_b[b] = y[i * block_rows : (i + 1) * block_rows].reshape(n, slots, 2 * hidden_width)
-
-    multiply([r], [h])
-    for k in range(1, n // 2 + 1):
-        ring_a.step(k)
-        ring_b.step(k)
-        ways = (0, 1) if k < n // 2 else (0,)
-        multiply([ring_a.block(w, k) for w in ways], [ring_b.block(w, k) for w in ways])
-
-    ring_h = Ring("head", h, n, lambda b, s: hidden.at[b, pl.ds(s * (n // 2), n // 2)], ring_h_sem)
-
-    def activate(b):
-        both = acc_a[b] + acc_b[:, b].reshape(block_rows, 2 * hidden_width)
-        gated, upward = both[:, :hidden_width], both[:, hidden_width:]
-        hidden[h, b] = (gated / (1.0 + jnp.exp(-gated)) * upward).astype(BF16)
-
-    for s in range(2):
-        for b in range(s * (n // 2), (s + 1) * (n // 2)):
-            activate(b)
-        ring_h.start(s)
     loads[5].wait()
-
-    def lower(b, s, first=False):
-        at = pl.ds(s * (n // 2), n // 2)
-        x = hidden[b, at].reshape(n // 2 * block_rows, hidden_width)
-        y = dot(x, down[pl.ds(pl.multiple_of(b * hidden_width, hidden_width), hidden_width), :])
-        y = y.reshape(n // 2, block_rows, width)
-        acc[at] = y if first else acc[at] + y
-
+    gather_step(0, 2)
+    gather_step(1, 1)
+    gather_step(0, 3)
+    gather_step(1, 2)
+    gather_step(0, 4)
+    activate(0)
+    gather_step(1, 3)
+    gather_step(1, 4)
     lower(h, 0, True)
+    hidden_step(0, 1)
+    activate(1)
+    hidden_step(0, 2)
     lower(h, 1, True)
-    for k in range(1, n // 2 + 1):
-        ring_h.step(k)
-        for s in range(2):
-            for way in (0, 1):
-                if s in ring_h.parts(way, k):
-                    lower(ring_h.block(way, k), s)
-
-    down_send[...] = acc[...].astype(BF16)
-    swap_down = Swap(
-        "req", r, n, lambda to: down_send.at[to], lambda at: down_recv.at[at], *down_sem
-    )
-    swap_down.start()
-    expert_rows = acc[r]
-    swap_down.wait_recv()
-    for d in range(1, n):
-        expert_rows += down_recv[lax.rem(r + d, n)].astype(F32)
-    back_send[...] = expert_rows.reshape(n, slots, width)
+    hidden_step(1, 1)
+    hidden_step(0, 3)
+    hidden_step(1, 2)
+    hidden_step(0, 4)
+    hand_over(0)
+    hidden_step(1, 3)
+    hidden_step(1, 4)
+    hand_over(1)
+
+    expert_rows = jnp.concatenate([collect(m) for m in range(micro)], axis=0)
+    sorted_rows = iota((micro * block_rows, micro * block_rows), 0)
+    sorted_rows = (
+        lax.rem(sorted_rows, slots) // SLOTS * block_rows
+        + sorted_rows // slots * SLOTS
+        + lax.rem(sorted_rows, SLOTS)
+        == iota((micro * block_rows, micro * block_rows), 1)
+    ).astype(BF16)
+    back_send[...] = dot(sorted_rows, expert_rows).reshape(n, slots, width)
 
     def back(to, at):
         return pltpu.make_async_remote_copy(
             src_ref=back_send.at[to],
             dst_ref=back_recv.at[at],
-            send_sem=back_sem[0].at[to],
-            recv_sem=back_sem[1].at[at],
+            send_sem=back_sem.at[0, to],
+            recv_sem=back_sem.at[1, at],
             device_id={"head": jnp.int32(to), "exp": h},
             device_id_type=MESH,
         )
@@ -442,13 +487,16 @@
         def _():
             back(j, j).wait_recv()
 
-    returned = back_recv[...].reshape(places, width).astype(BF16).astype(F32)
+    returned = back_recv[...].reshape(places, width)
     result = stream_all[e].astype(F32) + dot(mixing, returned, precision=EXACT)
     out_ref[...] = result.reshape(micro, group, width).astype(BF16)
 
-    for swap in (swap_att, swap_aux, swap_part, swap_stream, swap_a, swap_b, swap_down):
+    swaps = [swap_att, swap_aux, swap_part, swap_stream, *swaps_down]
+    for pair in first_swaps:
+        swaps += pair
+    for swap in swaps:
         swap.wait_send()
-    for ring in (ring_a, ring_b, ring_h):
+    for ring in rings_a + rings_b + rings_h:
         ring.wait_send()
     for j in range(n):
 
@@ -480,11 +528,8 @@
     smem = pl.BlockSpec(memory_space=pltpu.SMEM)
     anywhere = pl.BlockSpec(memory_space=pl.ANY)
 
-    def pair(count):
-        return (pltpu.SemaphoreType.DMA((count,)), pltpu.SemaphoreType.DMA((count,)))
-
-    ring = (pltpu.SemaphoreType.DMA((n - 1,)),) * 4
-    block_rows = n * slots
+    block_rows = n * SLOTS
+    all_rows = n * block_rows
     scratch = [
         pltpu.VMEM(cache_keys.shape, BF16),
         pltpu.VMEM(cache_values.shape, BF16),
@@ -497,30 +542,20 @@
         pltpu.VMEM((n, tokens, width), BF16),
         pltpu.VMEM((n, tokens, width), BF16),
         pltpu.VMEM((n, tokens, width), BF16),
-        pltpu.VMEM((n, 2 * slots, features // 4), BF16),
-        pltpu.VMEM((n, 2 * slots, features // 4), BF16),
-        pltpu.VMEM((n, block_rows, features // 2), BF16),
-        pltpu.VMEM((n, block_rows, features // 2), BF16),
-        pltpu.VMEM((n, block_rows, 2 * hidden_width), F32),
-        pltpu.VMEM((n, n, slots, 2 * hidden_width), F32),
-        pltpu.VMEM((n, n, block_rows, hidden_width), BF16),
-        pltpu.VMEM((n, block_rows, width), F32),
-        pltpu.VMEM((n, block_rows, width), BF16),
-        pltpu.VMEM((n, block_rows, width), BF16),
+        pltpu.VMEM((micro, n, n // 2 * SLOTS, width), BF16),
+        pltpu.VMEM((micro, n, n // 2 * SLOTS, width), BF16),
+        pltpu.VMEM((n, micro, block_rows, features // 2), BF16),
+        pltpu.VMEM((n, micro, block_rows, features // 2), BF16),
+        pltpu.VMEM((n, micro, all_rows, hidden_width), BF16),
+        pltpu.VMEM((micro, n, block_rows, width), F32),
+        pltpu.VMEM((micro, n, block_rows, width), BF16),
+        pltpu.VMEM((micro, n, block_rows, width), BF16),
         pltpu.VMEM((n, slots, width), F32),
         pltpu.VMEM((n, slots, width), F32),
         pltpu.SemaphoreType.DMA((6,)),
-        pair(n - 1),
-        pair(n - 1),
-        pair(n - 1),
-        pair(n - 1),
-        pair(n - 1),
-        pair(n - 1),
-        ring,
-        ring,
-        ring,
-        pair(n - 1),
-        pair(n),
+        pltpu.SemaphoreType.DMA((10, 2, n - 1)),
+        pltpu.SemaphoreType.DMA((3 * micro, 4, n // 2)),
+        pltpu.SemaphoreType.DMA((2, n)),
     ]
     return pl.pallas_call(
         functools.partial(layer, n),

time: 99.7 us -> 99.5 us (level)
  no operation moved by 1% of the time
where the time goes in v3:
time: 99.5 us; the launch traced here: 98.8 us
  Pallas kernels  97.4 us (98%)
  local copies, waits for them, and re-layouts  1.31 us (1%)
    pallas_call x1, Pallas kernels, per_device(): pl.pallas_call(functools.partial(layer, n), out_shape=jax.ShapeDtypeStruc...  97.4 us

profile of v3, /device:TPU:1, one launch (start us, length us, event | category | flops | bytes accessed | tf_op | source)
XLA Modules:
  0.0 98.8 jit_solution(14505443597041741959)
XLA Ops:
  0.0 97.4 %shard_map.118 = bf16[2,8,384]{2,1,0:T(8,128)(2,1)} custom-call(bf16[2,8,384]{2,1,0:T(8,128)(2,1)} %query_ref.1, bf16[2,8,32,128]{3,2,1,0:T(8,128)(2,1)} %keys_hbm.1, bf16[2,8,32,128]{3,2,1,0:T(8,128)(2,1)} %values_hbm.1, s32[2,8]{1,0:T(2,128)} %lengths_ref.1, bf16[384,384]{1,0:T(8,128)(2,1)} %proj_hbm.1, bf16[2,8,384]{2,1,0:T(8,128)(2,1)} %residual_ref.1, ...), custom_call_target="tpu_custom_call" | custom-call | tf_op jit(solution)/shard_map/pallas_call | solution.py:560
  97.5 1.3 %copy.14 = bf16[2,8,384]{2,1,0:T(8,128)(2,1)} copy(bf16[2,8,384]{2,1,0:T(8,128)(2,1)} %shard_map.118) | data formatting | bytes 24576

commit v4 on v3

--- a/solution.py
+++ b/solution.py
@@ -12,7 +12,6 @@
 SLOTS = 4
 F32 = jnp.float32
 BF16 = jnp.bfloat16
-EXACT = lax.Precision.HIGHEST
 
 
 def iota(shape, axis):
@@ -25,6 +24,13 @@
 
 def dot_t(a, b, **kw):
     return lax.dot_general(a, b, (((1,), (1,)), ((), ())), preferred_element_type=F32, **kw)
+
+
+def pieces(x):
+    high = x.astype(BF16)
+    rest = x - high.astype(F32)
+    middle = rest.astype(BF16)
+    return high, middle, (rest - middle.astype(F32)).astype(BF16)
 
 
 class Swap:
@@ -131,6 +137,10 @@
     first_b,
     rows_a,
     rows_b,
+    take_all,
+    ordered,
+    crossed,
+    sorted_rows,
     hidden,
     acc,
     down_send,
@@ -177,156 +187,178 @@
     for load in loads:
         load.start()
 
-    per_key = width // HEAD_DIM
-    queries = query_ref[...].astype(F32).reshape(tokens, width)
-    queries = jnp.concatenate(
-        [queries[:, j * HEAD_DIM : (j + 1) * HEAD_DIM] for j in range(per_key)], axis=0
-    ).astype(BF16)
-    columns = tokens * positions
-    owner = iota((1, columns), 1) // positions
-    limit = jnp.zeros((1, columns), jnp.int32)
-    for t in range(tokens):
-        limit = jnp.where(owner == t, lengths_ref[t // group, t % group], limit)
-    valid = lax.rem(iota((1, columns), 1), positions) < limit
-    owner = jnp.where(valid, owner, -1)
-    allowed = lax.rem(iota((per_key * tokens, columns), 0), tokens) == owner
-    loads[0].wait()
-    scores = dot_t(queries, keys[...].reshape(columns, HEAD_DIM)) * HEAD_DIM ** (-0.5)
-    scores = jnp.where(allowed, scores, F32(-1e30))
-    exponents = jnp.exp(scores - jnp.max(scores, axis=-1, keepdims=True))
-    weights = (exponents / jnp.sum(exponents, axis=-1, keepdims=True)).astype(BF16)
-    loads[1].wait()
-    mixed = dot(weights, values[...].reshape(columns, HEAD_DIM))
-    for j in range(per_key):
-        att_all[e, :, j * HEAD_DIM : (j + 1) * HEAD_DIM] = mixed[
-            j * tokens : (j + 1) * tokens
-        ].astype(BF16)
-    gain = jnp.broadcast_to(gain_ref[...].astype(F32).reshape(1, width), (n, width))
-    aux_all[e] = jnp.concatenate([router_ref[...].astype(F32), gain], axis=0).astype(BF16)
-
-    pl.semaphore_wait(barrier, 3 * (n - 1) + n - jnp.where(h == e, 1, 0))
+    with jax.named_scope("attention"):
+        per_key = width // HEAD_DIM
+        queries = query_ref[...].astype(F32).reshape(tokens, width)
+        queries = jnp.concatenate(
+            [queries[:, j * HEAD_DIM : (j + 1) * HEAD_DIM] for j in range(per_key)], axis=0
+        ).astype(BF16)
+        columns = tokens * positions
+        owner = iota((1, columns), 1) // positions
+        limit = jnp.zeros((1, columns), jnp.int32)
+        for t in range(tokens):
+            limit = jnp.where(owner == t, lengths_ref[t // group, t % group], limit)
+        valid = lax.rem(iota((1, columns), 1), positions) < limit
+        owner = jnp.where(valid, owner, -1)
+        allowed = lax.rem(iota((per_key * tokens, columns), 0), tokens) == owner
+        loads[0].wait()
+        scores = dot_t(queries, keys[...].reshape(columns, HEAD_DIM)) * HEAD_DIM ** (-0.5)
+        scores = jnp.where(allowed, scores, F32(-1e30))
+        exponents = jnp.exp(scores - jnp.max(scores, axis=-1, keepdims=True))
+        weights = (exponents / jnp.sum(exponents, axis=-1, keepdims=True)).astype(BF16)
+        loads[1].wait()
+        mixed = dot(weights, values[...].reshape(columns, HEAD_DIM))
+        for j in range(per_key):
+            att_all[e, :, j * HEAD_DIM : (j + 1) * HEAD_DIM] = mixed[
+                j * tokens : (j + 1) * tokens
+            ].astype(BF16)
+        gain = jnp.broadcast_to(gain_ref[...].astype(F32).reshape(1, width), (n, width))
+        aux_all[e] = jnp.concatenate([router_ref[...].astype(F32), gain], axis=0).astype(BF16)
+
+    with jax.named_scope("entry"):
+        pl.semaphore_wait(barrier, 3 * (n - 1) + n - jnp.where(h == e, 1, 0))
 
     swap_att = Swap("exp", e, n, lambda to: att_all.at[e], lambda at: att_all.at[at], swap_sem.at[0])
     swap_aux = Swap("exp", e, n, lambda to: aux_all.at[e], lambda at: aux_all.at[at], swap_sem.at[1])
     swap_att.start()
     swap_aux.start()
 
-    places = n * slots
-    diagonal = iota((group, group), 0) == iota((group, group), 1)
-
-    def upright(row):
-        return jnp.sum(jnp.where(diagonal, row, F32(0.0)), axis=-1, keepdims=True)
-
-    ids = [
-        jnp.concatenate(
-            [upright(ids_ref[m][k : k + 1, :].astype(F32)) for m in range(micro)], axis=0
-        ).astype(jnp.int32)
-        for k in range(2)
-    ]
-    token_at = iota((tokens, places), 0)
-    column = iota((tokens, places), 1)
-    hots = [(ids[k] == column // slots).astype(F32) for k in range(2)]
-    earlier_of = (
-        (iota((tokens, tokens), 1) < iota((tokens, tokens), 0))
-        & (iota((tokens, tokens), 1) // group == iota((tokens, tokens), 0) // group)
-    ).astype(BF16)
-    earlier = dot(earlier_of, (hots[0] + hots[1]).astype(BF16))
-    fits = (lax.rem(column, SLOTS).astype(F32) == earlier) & (
-        lax.rem(column, slots) // SLOTS == token_at // group
-    )
-    chosen_at = [jnp.where(fits, hot, F32(0.0)) for hot in hots]
-    sel_own = dot_t(
-        ((iota((slots, places), 1) - slots * e) == iota((slots, places), 0)).astype(BF16),
-        (chosen_at[0] + chosen_at[1]).astype(BF16),
-    ).astype(BF16)
-
-    loads[2].wait()
-    swap_att.wait_recv()
-    partial = dot(att_all[...].reshape(n * tokens, width), proj[...]).reshape(n, tokens, width)
-    part_own[...] = partial
-    part_send[...] = partial.astype(BF16)
-    swap_part = Swap(
-        "head", h, n, lambda to: part_send.at[to], lambda at: part_recv.at[at], swap_sem.at[2]
-    )
-    swap_part.start()
-    projected = part_own[h]
-    residual = residual_ref[...].astype(F32).reshape(tokens, width)
-    swap_part.wait_recv()
-    for d in range(1, n):
-        projected += part_recv[lax.rem(h + d, n)].astype(F32)
-    stream_all[e] = (residual + projected).astype(BF16)
-    swap_stream = Swap(
-        "exp", e, n, lambda to: stream_all.at[e], lambda at: stream_all.at[at], swap_sem.at[3]
-    )
-    swap_stream.start()
-    swap_aux.wait_recv()
-    swap_stream.wait_recv()
-
-    squares = jnp.zeros((tokens, width), F32)
-    for j in range(n):
-        block = stream_all[j].astype(F32)
-        squares += block * block
-    inverse = lax.rsqrt(jnp.sum(squares, axis=-1, keepdims=True) / features + 1e-05)
-    normed = []
-    for j in range(n):
-        full = stream_all[j].astype(F32) * aux_all[j].astype(F32)[n : n + 1] * inverse
-        normed.append(full)
-    chunks = n // 2
-    packed = chunks * SLOTS
-    stacked = [
-        jnp.concatenate([full.astype(BF16) for full in normed[i * chunks : (i + 1) * chunks]], axis=0)
-        for i in range(2)
-    ]
-    first_swaps = []
-    for m in range(micro):
-        pick = (
-            iota((packed, slots), 1) == m * SLOTS + lax.rem(iota((packed, slots), 0), SLOTS)
+    with jax.named_scope("routing"):
+        places = n * slots
+        diagonal = iota((group, group), 0) == iota((group, group), 1)
+
+        def upright(row):
+            return jnp.sum(jnp.where(diagonal, row, F32(0.0)), axis=-1, keepdims=True)
+
+        ids = [
+            jnp.concatenate(
+                [upright(ids_ref[m][k : k + 1, :].astype(F32)) for m in range(micro)], axis=0
+            ).astype(jnp.int32)
+            for k in range(2)
+        ]
+        token_at = iota((tokens, places), 0)
+        column = iota((tokens, places), 1)
+        hots = [(ids[k] == column // slots).astype(F32) for k in range(2)]
+        earlier_of = (
+            (iota((tokens, tokens), 1) < iota((tokens, tokens), 0))
+            & (iota((tokens, tokens), 1) // group == iota((tokens, tokens), 0) // group)
         ).astype(BF16)
-        spread = (
-            lax.rem(iota((tokens, chunks * tokens), 1), tokens)
-            == iota((tokens, chunks * tokens), 0)
+        earlier = dot(earlier_of, (hots[0] + hots[1]).astype(BF16))
+        fits = (lax.rem(column, SLOTS).astype(F32) == earlier) & (
+            lax.rem(column, slots) // SLOTS == token_at // group
+        )
+        chosen_at = [jnp.where(fits, hot, F32(0.0)) for hot in hots]
+        sel_own = dot_t(
+            ((iota((slots, places), 1) - slots * e) == iota((slots, places), 0)).astype(BF16),
+            (chosen_at[0] + chosen_at[1]).astype(BF16),
         ).astype(BF16)
-        same = (
-            iota((packed, chunks * tokens), 0) // SLOTS
-            == iota((packed, chunks * tokens), 1) // tokens
-        )
-        take = dot(dot(pick, sel_own).astype(BF16), spread)
-        take = jnp.where(same, take, F32(0.0)).astype(BF16)
-        first_a[m, h] = dot(take, stacked[0]).astype(BF16)
-        first_b[m, r] = dot(take, stacked[1]).astype(BF16)
-        swap_a = Swap(
-            "head",
-            h,
-            n,
-            lambda to, m=m: first_a.at[m, h],
-            lambda at, m=m: first_a.at[m, at],
-            swap_sem.at[4 + 2 * m],
-        )
-        swap_b = Swap(
-            "req",
-            r,
-            n,
-            lambda to, m=m: first_b.at[m, r],
-            lambda at, m=m: first_b.at[m, at],
-            swap_sem.at[5 + 2 * m],
-        )
-        swap_a.start()
-        swap_b.start()
-        first_swaps.append((swap_a, swap_b))
+
+        chunks = n // 2
+        packed = chunks * SLOTS
+        block_rows = n * SLOTS
+        all_rows = n * block_rows
+        for m in range(micro):
+            pick = (
+                iota((packed, slots), 1) == m * SLOTS + lax.rem(iota((packed, slots), 0), SLOTS)
+            ).astype(BF16)
+            spread = (
+                lax.rem(iota((tokens, chunks * tokens), 1), tokens)
+                == iota((tokens, chunks * tokens), 0)
+            ).astype(BF16)
+            same = (
+                iota((packed, chunks * tokens), 0) // SLOTS
+                == iota((packed, chunks * tokens), 1) // tokens
+            )
+            take = dot(dot(pick, sel_own).astype(BF16), spread)
+            take_all[m] = jnp.where(same, take, F32(0.0)).astype(BF16)
+
+        def one_hot(size, place):
+            return (place(iota((size, size), 0)) == iota((size, size), 1)).astype(BF16)
+
+        ordered[...] = one_hot(
+            n * packed,
+            lambda i: lax.rem(i, block_rows) // SLOTS * packed
+            + i // block_rows * SLOTS
+            + lax.rem(i, SLOTS),
+        )
+        crossed[...] = one_hot(
+            all_rows,
+            lambda i: lax.rem(i, block_rows) // SLOTS * block_rows
+            + i // block_rows * SLOTS
+            + lax.rem(i, SLOTS),
+        )
+        sorted_rows[...] = one_hot(
+            micro * block_rows,
+            lambda i: lax.rem(i, slots) // SLOTS * block_rows + i // slots * SLOTS + lax.rem(i, SLOTS),
+        )
+
+    with jax.named_scope("projection"):
+        loads[2].wait()
+        swap_att.wait_recv()
+        partial = dot(att_all[...].reshape(n * tokens, width), proj[...]).reshape(n, tokens, width)
+        part_own[...] = partial
+        part_send[...] = partial.astype(BF16)
+        swap_part = Swap(
+            "head", h, n, lambda to: part_send.at[to], lambda at: part_recv.at[at], swap_sem.at[2]
+        )
+        swap_part.start()
+    with jax.named_scope("stream"):
+        projected = part_own[h]
+        residual = residual_ref[...].astype(F32).reshape(tokens, width)
+        swap_part.wait_recv()
+        for d in range(1, n):
+            projected += part_recv[lax.rem(h + d, n)].astype(F32)
+        stream_all[e] = (residual + projected).astype(BF16)
+        swap_stream = Swap(
+            "exp", e, n, lambda to: stream_all.at[e], lambda at: stream_all.at[at], swap_sem.at[3]
+        )
+        swap_stream.start()
+    with jax.named_scope("norm"):
+        swap_aux.wait_recv()
+        swap_stream.wait_recv()
+
+        squares = jnp.zeros((tokens, width), F32)
+        for j in range(n):
+            block = stream_all[j].astype(F32)
+            squares += block * block
+        inverse = lax.rsqrt(jnp.sum(squares, axis=-1, keepdims=True) / features + 1e-05)
+        normed = []
+        for j in range(n):
+            full = stream_all[j].astype(F32) * aux_all[j].astype(F32)[n : n + 1] * inverse
+            normed.append(full)
+        stacked = [
+            jnp.concatenate([full.astype(BF16) for full in normed[i * chunks : (i + 1) * chunks]], axis=0)
+            for i in range(2)
+        ]
+        first_swaps = []
+        for m in range(micro):
+            take = take_all[m]
+            first_a[m, h] = dot(take, stacked[0]).astype(BF16)
+            first_b[m, r] = dot(take, stacked[1]).astype(BF16)
+            swap_a = Swap(
+                "head",
+                h,
+                n,
+                lambda to, m=m: first_a.at[m, h],
+                lambda at, m=m: first_a.at[m, at],
+                swap_sem.at[4 + 2 * m],
+            )
+            swap_b = Swap(
+                "req",
+                r,
+                n,
+                lambda to, m=m: first_b.at[m, r],
+                lambda at, m=m: first_b.at[m, at],
+                swap_sem.at[5 + 2 * m],
+            )
+            swap_a.start()
+            swap_b.start()
+            first_swaps.append((swap_a, swap_b))
 
     half = features // 2
-    block_rows = n * SLOTS
-    all_rows = n * block_rows
-    ordered = iota((n * packed, n * packed), 0)
-    ordered = (
-        lax.rem(ordered, block_rows) // SLOTS * packed
-        + ordered // block_rows * SLOTS
-        + lax.rem(ordered, SLOTS)
-        == iota((n * packed, n * packed), 1)
-    ).astype(BF16)
 
     def settle(first, rows_to):
-        y = dot(ordered, first[...].reshape(n * packed, width)).astype(BF16)
+        y = dot(ordered[...], first[...].reshape(n * packed, width)).astype(BF16)
         for c in range(chunks):
             rows_to[:, pl.ds(c * width, width)] = y[c * block_rows : (c + 1) * block_rows]
 
@@ -350,36 +382,32 @@
         first_swaps[m][1].wait_recv()
         settle(first_b.at[m], rows_b.at[h, m])
 
-    settle_a(0)
-    rings_a[0].start()
-    settle_b(0)
-    rings_b[0].start()
-    settle_a(1)
-    settle_b(1)
-
-    logits = jnp.zeros((tokens, 2 * n), F32)
-    for j in range(n):
-        logits += dot_t(normed[j], aux_all[j].astype(F32), precision=EXACT)
-    lane = iota((tokens, 2 * n), 1)
-    powers = [
-        jnp.exp(jnp.sum(jnp.where(lane == ids[k], logits, F32(0.0)), axis=-1, keepdims=True))
-        for k in range(2)
-    ]
-    total = powers[0] + powers[1]
-    mixing = powers[0] / total * chosen_at[0] + powers[1] / total * chosen_at[1]
-
-    crossed = iota((all_rows, all_rows), 0)
-    crossed = (
-        lax.rem(crossed, block_rows) // SLOTS * block_rows
-        + crossed // block_rows * SLOTS
-        + lax.rem(crossed, SLOTS)
-        == iota((all_rows, all_rows), 1)
-    ).astype(BF16)
+    with jax.named_scope("settle"):
+        settle_a(0)
+        rings_a[0].start()
+        settle_b(0)
+        rings_b[0].start()
+        settle_a(1)
+        settle_b(1)
+
+    def mix():
+        logits = jnp.zeros((tokens, 2 * n), F32)
+        for j in range(n):
+            full = stream_all[j].astype(F32) * aux_all[j].astype(F32)[n : n + 1] * inverse
+            for piece in pieces(full):
+                logits += dot_t(piece, aux_all[j])
+        lane = iota((tokens, 2 * n), 1)
+        powers = [
+            jnp.exp(jnp.sum(jnp.where(lane == ids[k], logits, F32(0.0)), axis=-1, keepdims=True))
+            for k in range(2)
+        ]
+        total = powers[0] + powers[1]
+        return powers[0] / total * chosen_at[0] + powers[1] / total * chosen_at[1]
 
     def activate(m):
         x = rows_a[:, m].reshape(all_rows, half)
         y = dot(x, wide[pl.ds(0, half), :])
-        x = dot(crossed, rows_b[:, m].reshape(all_rows, half)).astype(BF16)
+        x = dot(crossed[...], rows_b[:, m].reshape(all_rows, half)).astype(BF16)
         y += dot(x, wide[pl.ds(half, half), :])
         gated, upward = y[:, :hidden_width], y[:, hidden_width:]
         hidden[h, m] = (gated / (1.0 + jnp.exp(-gated)) * upward).astype(BF16)
@@ -423,43 +451,45 @@
             total += down_recv[m, lax.rem(r + d, n)].astype(F32)
         return total.astype(BF16)
 
-    gather_step(0, 1)
-    rings_a[1].start()
-    rings_b[1].start()
-    loads[3].wait()
-    loads[4].wait()
-    loads[5].wait()
-    gather_step(0, 2)
-    gather_step(1, 1)
-    gather_step(0, 3)
-    gather_step(1, 2)
-    gather_step(0, 4)
-    activate(0)
-    gather_step(1, 3)
-    gather_step(1, 4)
-    lower(h, 0, True)
-    hidden_step(0, 1)
-    activate(1)
-    hidden_step(0, 2)
-    lower(h, 1, True)
-    hidden_step(1, 1)
-    hidden_step(0, 3)
-    hidden_step(1, 2)
-    hidden_step(0, 4)
-    hand_over(0)
-    hidden_step(1, 3)
-    hidden_step(1, 4)
-    hand_over(1)
-
-    expert_rows = jnp.concatenate([collect(m) for m in range(micro)], axis=0)
-    sorted_rows = iota((micro * block_rows, micro * block_rows), 0)
-    sorted_rows = (
-        lax.rem(sorted_rows, slots) // SLOTS * block_rows
-        + sorted_rows // slots * SLOTS
-        + lax.rem(sorted_rows, SLOTS)
-        == iota((micro * block_rows, micro * block_rows), 1)
-    ).astype(BF16)
-    back_send[...] = dot(sorted_rows, expert_rows).reshape(n, slots, width)
+    with jax.named_scope("rows_first"):
+        gather_step(0, 1)
+        rings_a[1].start()
+        rings_b[1].start()
+        loads[3].wait()
+        loads[4].wait()
+        loads[5].wait()
+    with jax.named_scope("rows_rest"):
+        gather_step(0, 2)
+        gather_step(1, 1)
+        gather_step(0, 3)
+        gather_step(1, 2)
+        gather_step(0, 4)
+    with jax.named_scope("activate_first"):
+        activate(0)
+    with jax.named_scope("rows_last"):
+        gather_step(1, 3)
+        gather_step(1, 4)
+    with jax.named_scope("hidden_first"):
+        lower(h, 0, True)
+        hidden_step(0, 1)
+    with jax.named_scope("activate_second"):
+        activate(1)
+    with jax.named_scope("hidden_rest"):
+        hidden_step(0, 2)
+        mixing = mix()
+        lower(h, 1, True)
+        hidden_step(1, 1)
+        hidden_step(0, 3)
+        hidden_step(1, 2)
+        hidden_step(0, 4)
+        hand_over(0)
+        hidden_step(1, 3)
+        hidden_step(1, 4)
+        hand_over(1)
+
+    with jax.named_scope("collect"):
+        expert_rows = jnp.concatenate([collect(m) for m in range(micro)], axis=0)
+        back_send[...] = dot(sorted_rows[...], expert_rows).reshape(n, slots, width)
 
     def back(to, at):
         return pltpu.make_async_remote_copy(
@@ -471,24 +501,28 @@
             device_id_type=MESH,
         )
 
-    for j in range(n):
-
-        @pl.when(jnp.logical_or(h != e, h != j))
-        def _():
-            back(j, e).start()
-
-        @pl.when(jnp.logical_and(h == e, h == j))
-        def _():
-            back_recv[j] = back_send[j]
-
-    for j in range(n):
-
-        @pl.when(jnp.logical_or(h != e, e != j))
-        def _():
-            back(j, j).wait_recv()
+    with jax.named_scope("return"):
+        for j in range(n):
+
+            @pl.when(jnp.logical_or(h != e, h != j))
+            def _():
+                back(j, e).start()
+
+            @pl.when(jnp.logical_and(h == e, h == j))
+            def _():
+                back_recv[j] = back_send[j]
+
+        for j in range(n):
+
+            @pl.when(jnp.logical_or(h != e, e != j))
+            def _():
+                back(j, j).wait_recv()
 
     returned = back_recv[...].reshape(places, width)
-    result = stream_all[e].astype(F32) + dot(mixing, returned, precision=EXACT)
+    returned = returned.astype(BF16)
+    result = stream_all[e].astype(F32)
+    for piece in pieces(mixing):
+        result += dot(piece, returned)
     out_ref[...] = result.reshape(micro, group, width).astype(BF16)
 
     swaps = [swap_att, swap_aux, swap_part, swap_stream, *swaps_down]
@@ -546,6 +580,10 @@
         pltpu.VMEM((micro, n, n // 2 * SLOTS, width), BF16),
         pltpu.VMEM((n, micro, block_rows, features // 2), BF16),
         pltpu.VMEM((n, micro, block_rows, features // 2), BF16),
+        pltpu.VMEM((micro, n // 2 * SLOTS, n // 2 * tokens), BF16),
+        pltpu.VMEM((n * n // 2 * SLOTS, n * n // 2 * SLOTS), BF16),
+        pltpu.VMEM((all_rows, all_rows), BF16),
+        pltpu.VMEM((micro * block_rows, micro * block_rows), BF16),
         pltpu.VMEM((n, micro, all_rows, hidden_width), BF16),
         pltpu.VMEM((micro, n, block_rows, width), F32),
         pltpu.VMEM((micro, n, block_rows, width), BF16),

time: 99.5 us -> 100 us (level)
  Pallas kernels: 97.4 us -> 98.7 us
    pallas_call x1, Pallas kernels: 97.4 us -> 98.7 us  [per_device(): pl.pallas_call(functools.partial(layer, n), out_shape=jax.ShapeDtypeStruc...]
where the time goes in v4:
time: 100 us
  Pallas kernels  98.7 us (99%)
  local copies, waits for them, and re-layouts  1.31 us (1%)
    pallas_call x1, Pallas kernels, per_device(): pl.pallas_call(functools.partial(layer, n), out_shape=jax.ShapeDtypeStruc...  98.7 us

profile of v4, /device:TPU:1, one launch (start us, length us, event | category | flops | bytes accessed | tf_op | source)
XLA Modules:
  0.0 100.0 jit_solution(6870487961402088457)
XLA Ops:
  0.0 98.7 %shard_map.118 = bf16[2,8,384]{2,1,0:T(8,128)(2,1)} custom-call(bf16[2,8,384]{2,1,0:T(8,128)(2,1)} %query_ref.1, bf16[2,8,32,128]{3,2,1,0:T(8,128)(2,1)} %keys_hbm.1, bf16[2,8,32,128]{3,2,1,0:T(8,128)(2,1)} %values_hbm.1, s32[2,8]{1,0:T(2,128)} %lengths_ref.1, bf16[384,384]{1,0:T(8,128)(2,1)} %proj_hbm.1, bf16[2,8,384]{2,1,0:T(8,128)(2,1)} %residual_ref.1, ...), custom_call_target="tpu_custom_call" | custom-call | tf_op jit(solution)/shard_map/pallas_call | solution.py:598
  98.7 1.3 %copy.14 = bf16[2,8,384]{2,1,0:T(8,128)(2,1)} copy(bf16[2,8,384]{2,1,0:T(8,128)(2,1)} %shard_map.118) | data formatting | bytes 24576

commit v5 on v4

--- a/solution.py
+++ b/solution.py
@@ -35,31 +35,32 @@
 
 class Swap:
     def __init__(self, axis, me, n, src, dst, sems):
-        self.axis, self.me, self.n, self.src, self.dst = axis, me, n, src, dst
-        self.sems = sems
-
-    def copy(self, d, to, at):
+        self.axis, self.me, self.n, self.src, self.dst, self.sems = axis, me, n, src, dst, sems
+
+    def copy(self, src, dst, to):
         return pltpu.make_async_remote_copy(
-            src_ref=self.src(to),
-            dst_ref=self.dst(at),
-            send_sem=self.sems.at[0, d - 1],
-            recv_sem=self.sems.at[1, d - 1],
+            src_ref=src,
+            dst_ref=dst,
+            send_sem=self.sems.at[0],
+            recv_sem=self.sems.at[1],
             device_id={self.axis: to},
             device_id_type=MESH,
         )
 
     def start(self):
-        for d in range(1, self.n):
-            self.copy(d, lax.rem(self.me + d, self.n), self.me).start()
+        for d in sorted(range(1, self.n), key=lambda d: -min(d, self.n - d)):
+            to = lax.rem(self.me + d, self.n)
+            self.copy(self.src(to), self.dst.at[self.me], to).start()
+
+    def everything(self):
+        others = self.dst.at[pl.ds(0, self.n - 1)]
+        return self.copy(others, others, lax.rem(self.me + 1, self.n))
 
     def wait_recv(self):
-        for d in range(1, self.n):
-            source = lax.rem(self.me + self.n - d, self.n)
-            self.copy(d, source, source).wait_recv()
+        self.everything().wait_recv()
 
     def wait_send(self):
-        for d in range(1, self.n):
-            self.copy(d, lax.rem(self.me + d, self.n), self.me).wait_send()
+        self.everything().wait_send()
 
 
 class Ring:
@@ -218,8 +219,8 @@
     with jax.named_scope("entry"):
         pl.semaphore_wait(barrier, 3 * (n - 1) + n - jnp.where(h == e, 1, 0))
 
-    swap_att = Swap("exp", e, n, lambda to: att_all.at[e], lambda at: att_all.at[at], swap_sem.at[0])
-    swap_aux = Swap("exp", e, n, lambda to: aux_all.at[e], lambda at: aux_all.at[at], swap_sem.at[1])
+    swap_att = Swap("exp", e, n, lambda to: att_all.at[e], att_all, swap_sem.at[0])
+    swap_aux = Swap("exp", e, n, lambda to: aux_all.at[e], aux_all, swap_sem.at[1])
     swap_att.start()
     swap_aux.start()
 
@@ -299,7 +300,7 @@
         part_own[...] = partial
         part_send[...] = partial.astype(BF16)
         swap_part = Swap(
-            "head", h, n, lambda to: part_send.at[to], lambda at: part_recv.at[at], swap_sem.at[2]
+            "head", h, n, lambda to: part_send.at[to], part_recv, swap_sem.at[2]
         )
         swap_part.start()
     with jax.named_scope("stream"):
@@ -310,7 +311,7 @@
             projected += part_recv[lax.rem(h + d, n)].astype(F32)
         stream_all[e] = (residual + projected).astype(BF16)
         swap_stream = Swap(
-            "exp", e, n, lambda to: stream_all.at[e], lambda at: stream_all.at[at], swap_sem.at[3]
+            "exp", e, n, lambda to: stream_all.at[e], stream_all, swap_sem.at[3]
         )
         swap_stream.start()
     with jax.named_scope("norm"):
@@ -340,7 +341,7 @@
                 h,
                 n,
                 lambda to, m=m: first_a.at[m, h],
-                lambda at, m=m: first_a.at[m, at],
+                first_a.at[m],
                 swap_sem.at[4 + 2 * m],
             )
             swap_b = Swap(
@@ -348,7 +349,7 @@
                 r,
                 n,
                 lambda to, m=m: first_b.at[m, r],
-                lambda at, m=m: first_b.at[m, at],
+                first_b.at[m],
                 swap_sem.at[5 + 2 * m],
             )
             swap_a.start()
@@ -434,7 +435,7 @@
             r,
             n,
             lambda to, m=m: down_send.at[m, to],
-            lambda at, m=m: down_recv.at[m, at],
+            down_recv.at[m],
             swap_sem.at[8 + m],
         )
         for m in range(micro)
@@ -455,37 +456,41 @@
         gather_step(0, 1)
         rings_a[1].start()
         rings_b[1].start()
-        loads[3].wait()
-        loads[4].wait()
-        loads[5].wait()
+        for load in loads[3:]:
+            load.wait()
+        for swap in (swap_att, swap_aux, swap_part, swap_stream):
+            swap.wait_send()
     with jax.named_scope("rows_rest"):
         gather_step(0, 2)
         gather_step(1, 1)
         gather_step(0, 3)
         gather_step(1, 2)
         gather_step(0, 4)
-    with jax.named_scope("activate_first"):
         activate(0)
-    with jax.named_scope("rows_last"):
         gather_step(1, 3)
+        lower(h, 0, True)
+        for pair in first_swaps:
+            for swap in pair:
+                swap.wait_send()
         gather_step(1, 4)
-    with jax.named_scope("hidden_first"):
-        lower(h, 0, True)
+    with jax.named_scope("hidden_units"):
         hidden_step(0, 1)
-    with jax.named_scope("activate_second"):
         activate(1)
-    with jax.named_scope("hidden_rest"):
         hidden_step(0, 2)
-        mixing = mix()
         lower(h, 1, True)
         hidden_step(1, 1)
+        mixing = mix()
         hidden_step(0, 3)
         hidden_step(1, 2)
+        for ring in rings_a + rings_b:
+            ring.wait_send()
         hidden_step(0, 4)
         hand_over(0)
         hidden_step(1, 3)
         hidden_step(1, 4)
         hand_over(1)
+        for ring in rings_h:
+            ring.wait_send()
 
     with jax.named_scope("collect"):
         expert_rows = jnp.concatenate([collect(m) for m in range(micro)], axis=0)
@@ -495,8 +500,8 @@
         return pltpu.make_async_remote_copy(
             src_ref=back_send.at[to],
             dst_ref=back_recv.at[at],
-            send_sem=back_sem.at[0, to],
-            recv_sem=back_sem.at[1, at],
+            send_sem=back_sem.at[0],
+            recv_sem=back_sem.at[1],
             device_id={"head": jnp.int32(to), "exp": h},
             device_id_type=MESH,
         )
@@ -512,11 +517,23 @@
             def _():
                 back_recv[j] = back_send[j]
 
-        for j in range(n):
-
-            @pl.when(jnp.logical_or(h != e, e != j))
+        for swap in swaps_down:
+            swap.wait_send()
+        for count, here in ((n, h != e), (n - 1, h == e)):
+
+            @pl.when(here)
             def _():
-                back(j, j).wait_recv()
+                those = back_recv.at[pl.ds(0, count)]
+                every = pltpu.make_async_remote_copy(
+                    src_ref=those,
+                    dst_ref=those,
+                    send_sem=back_sem.at[0],
+                    recv_sem=back_sem.at[1],
+                    device_id={"exp": lax.rem(e + 1, n)},
+                    device_id_type=MESH,
+                )
+                every.wait_recv()
+                every.wait_send()
 
     returned = back_recv[...].reshape(places, width)
     returned = returned.astype(BF16)
@@ -524,19 +541,6 @@
     for piece in pieces(mixing):
         result += dot(piece, returned)
     out_ref[...] = result.reshape(micro, group, width).astype(BF16)
-
-    swaps = [swap_att, swap_aux, swap_part, swap_stream, *swaps_down]
-    for pair in first_swaps:
-        swaps += pair
-    for swap in swaps:
-        swap.wait_send()
-    for ring in rings_a + rings_b + rings_h:
-        ring.wait_send()
-    for j in range(n):
-
-        @pl.when(jnp.logical_or(h != e, h != j))
-        def _():
-            back(j, e).wait_send()
 
 
 def per_device(
@@ -591,9 +595,9 @@
         pltpu.VMEM((n, slots, width), F32),
         pltpu.VMEM((n, slots, width), F32),
         pltpu.SemaphoreType.DMA((6,)),
-        pltpu.SemaphoreType.DMA((10, 2, n - 1)),
+        pltpu.SemaphoreType.DMA((10, 2)),
         pltpu.SemaphoreType.DMA((3 * micro, 4, n // 2)),
-        pltpu.SemaphoreType.DMA((2, n)),
+        pltpu.SemaphoreType.DMA((2,)),
     ]
     return pl.pallas_call(
         functools.partial(layer, n),

time: 100 us -> 94.8 us (0.948)
  Pallas kernels: 98.7 us -> 93.1 us
    pallas_call x1, Pallas kernels: 98.7 us -> 93.1 us  [per_device(): pl.pallas_call(functools.partial(layer, n), out_shape=jax.ShapeDtypeStruc...]
where the time goes in v5:
time: 94.8 us; the launch traced here: 94.5 us
  Pallas kernels  93.1 us (98%)
  local copies, waits for them, and re-layouts  1.31 us (1%)
    pallas_call x1, Pallas kernels, per_device(): pl.pallas_call(functools.partial(layer, n), out_shape=jax.ShapeDtypeStruc...  93.1 us

profile of v5, /device:TPU:1, one launch (start us, length us, event | category | flops | bytes accessed | tf_op | source)
XLA Modules:
  0.0 94.5 jit_solution(12511926920929659868)
XLA Ops:
  0.0 93.1 %shard_map.118 = bf16[2,8,384]{2,1,0:T(8,128)(2,1)} custom-call(bf16[2,8,384]{2,1,0:T(8,128)(2,1)} %query_ref.1, bf16[2,8,32,128]{3,2,1,0:T(8,128)(2,1)} %keys_hbm.1, bf16[2,8,32,128]{3,2,1,0:T(8,128)(2,1)} %values_hbm.1, s32[2,8]{1,0:T(2,128)} %lengths_ref.1, bf16[384,384]{1,0:T(8,128)(2,1)} %proj_hbm.1, bf16[2,8,384]{2,1,0:T(8,128)(2,1)} %residual_ref.1, ...), custom_call_target="tpu_custom_call" | custom-call | tf_op jit(solution)/shard_map/pallas_call | solution.py:602
  93.2 1.3 %copy.14 = bf16[2,8,384]{2,1,0:T(8,128)(2,1)} copy(bf16[2,8,384]{2,1,0:T(8,128)(2,1)} %shard_map.118) | data formatting | bytes 24576

commit v6 on v5

--- a/solution.py
+++ b/solution.py
@@ -136,9 +136,12 @@
     stream_all,
     first_a,
     first_b,
+    first_w,
     rows_a,
     rows_b,
-    take_all,
+    rows_w,
+    take_half,
+    take_whole,
     ordered,
     crossed,
     sorted_rows,
@@ -258,20 +261,20 @@
         packed = chunks * SLOTS
         block_rows = n * SLOTS
         all_rows = n * block_rows
-        for m in range(micro):
+        def taking(m, parts):
+            shape = (parts * SLOTS, parts * tokens)
             pick = (
-                iota((packed, slots), 1) == m * SLOTS + lax.rem(iota((packed, slots), 0), SLOTS)
+                iota((shape[0], slots), 1) == m * SLOTS + lax.rem(iota((shape[0], slots), 0), SLOTS)
             ).astype(BF16)
             spread = (
-                lax.rem(iota((tokens, chunks * tokens), 1), tokens)
-                == iota((tokens, chunks * tokens), 0)
+                lax.rem(iota((tokens, shape[1]), 1), tokens) == iota((tokens, shape[1]), 0)
             ).astype(BF16)
-            same = (
-                iota((packed, chunks * tokens), 0) // SLOTS
-                == iota((packed, chunks * tokens), 1) // tokens
-            )
-            take = dot(dot(pick, sel_own).astype(BF16), spread)
-            take_all[m] = jnp.where(same, take, F32(0.0)).astype(BF16)
+            same = iota(shape, 0) // SLOTS == iota(shape, 1) // tokens
+            table = dot(dot(pick, sel_own).astype(BF16), spread)
+            return jnp.where(same, table, F32(0.0)).astype(BF16)
+
+        take_half[...] = taking(0, chunks)
+        take_whole[...] = taking(1, n)
 
         def one_hot(size, place):
             return (place(iota((size, size), 0)) == iota((size, size), 1)).astype(BF16)
@@ -331,65 +334,38 @@
             jnp.concatenate([full.astype(BF16) for full in normed[i * chunks : (i + 1) * chunks]], axis=0)
             for i in range(2)
         ]
-        first_swaps = []
-        for m in range(micro):
-            take = take_all[m]
-            first_a[m, h] = dot(take, stacked[0]).astype(BF16)
-            first_b[m, r] = dot(take, stacked[1]).astype(BF16)
-            swap_a = Swap(
-                "head",
-                h,
-                n,
-                lambda to, m=m: first_a.at[m, h],
-                first_a.at[m],
-                swap_sem.at[4 + 2 * m],
-            )
-            swap_b = Swap(
-                "req",
-                r,
-                n,
-                lambda to, m=m: first_b.at[m, r],
-                first_b.at[m],
-                swap_sem.at[5 + 2 * m],
-            )
-            swap_a.start()
-            swap_b.start()
-            first_swaps.append((swap_a, swap_b))
+        first_a[h] = dot(take_half[...], stacked[0]).astype(BF16)
+        first_b[r] = dot(take_half[...], stacked[1]).astype(BF16)
+        swap_a = Swap("head", h, n, lambda to: first_a.at[h], first_a, swap_sem.at[4])
+        swap_b = Swap("req", r, n, lambda to: first_b.at[r], first_b, swap_sem.at[5])
+        swap_w = Swap("head", h, n, lambda to: first_w.at[h], first_w, swap_sem.at[6])
+        swap_a.start()
+        swap_b.start()
+        first_w[h] = dot(take_whole[...], jnp.concatenate(stacked, axis=0)).astype(BF16)
+        swap_w.start()
 
     half = features // 2
 
-    def settle(first, rows_to):
-        y = dot(ordered[...], first[...].reshape(n * packed, width)).astype(BF16)
-        for c in range(chunks):
+    def settle(swap, order, first, rows_to):
+        swap.wait_recv()
+        y = dot(order[...], first[...].reshape(n * first.shape[1], width)).astype(BF16)
+        for c in range(first.shape[1] // SLOTS):
             rows_to[:, pl.ds(c * width, width)] = y[c * block_rows : (c + 1) * block_rows]
 
-    rings_a = [
-        Ring("req", r, n, lambda b, m=m: rows_a.at[b, m], ring_sem.at[m]) for m in range(micro)
-    ]
-    rings_b = [
-        Ring("head", h, n, lambda b, m=m: rows_b.at[b, m], ring_sem.at[micro + m])
+    ring_a = Ring("req", r, n, lambda b: rows_a.at[b], ring_sem.at[0])
+    ring_b = Ring("head", h, n, lambda b: rows_b.at[b], ring_sem.at[1])
+    ring_w = Ring("req", r, n, lambda b: rows_w.at[b], ring_sem.at[2])
+    rings_h = [
+        Ring("head", h, n, lambda b, m=m: hidden.at[b, m], ring_sem.at[3 + m])
         for m in range(micro)
     ]
-    rings_h = [
-        Ring("head", h, n, lambda b, m=m: hidden.at[b, m], ring_sem.at[2 * micro + m])
-        for m in range(micro)
-    ]
-
-    def settle_a(m):
-        first_swaps[m][0].wait_recv()
-        settle(first_a.at[m], rows_a.at[r, m])
-
-    def settle_b(m):
-        first_swaps[m][1].wait_recv()
-        settle(first_b.at[m], rows_b.at[h, m])
 
     with jax.named_scope("settle"):
-        settle_a(0)
-        rings_a[0].start()
-        settle_b(0)
-        rings_b[0].start()
-        settle_a(1)
-        settle_b(1)
+        settle(swap_a, ordered, first_a, rows_a.at[r])
+        ring_a.start()
+        settle(swap_b, ordered, first_b, rows_b.at[h])
+        ring_b.start()
+        settle(swap_w, crossed, first_w, rows_w.at[r])
 
     def mix():
         logits = jnp.zeros((tokens, 2 * n), F32)
@@ -406,10 +382,12 @@
         return powers[0] / total * chosen_at[0] + powers[1] / total * chosen_at[1]
 
     def activate(m):
-        x = rows_a[:, m].reshape(all_rows, half)
-        y = dot(x, wide[pl.ds(0, half), :])
-        x = dot(crossed[...], rows_b[:, m].reshape(all_rows, half)).astype(BF16)
-        y += dot(x, wide[pl.ds(half, half), :])
+        if m == 0:
+            y = dot(rows_a[...].reshape(all_rows, half), wide[pl.ds(0, half), :])
+            x = dot(crossed[...], rows_b[...].reshape(all_rows, half)).astype(BF16)
+            y += dot(x, wide[pl.ds(half, half), :])
+        else:
+            y = dot(rows_w[...].reshape(all_rows, features), wide[...])
         gated, upward = y[:, :hidden_width], y[:, hidden_width:]
         hidden[h, m] = (gated / (1.0 + jnp.exp(-gated)) * upward).astype(BF16)
         rings_h[m].start()
@@ -420,9 +398,9 @@
         ).reshape(n, block_rows, width)
         acc[m] = y if first else acc[m] + y
 
-    def gather_step(m, k):
-        rings_a[m].step(k)
-        rings_b[m].step(k)
+    def gather_step(k):
+        ring_a.step(k)
+        ring_b.step(k)
 
     def hidden_step(m, k):
         rings_h[m].step(k)
@@ -436,7 +414,7 @@
             n,
             lambda to, m=m: down_send.at[m, to],
             down_recv.at[m],
-            swap_sem.at[8 + m],
+            swap_sem.at[7 + m],
         )
         for m in range(micro)
     ]
@@ -452,48 +430,46 @@
             total += down_recv[m, lax.rem(r + d, n)].astype(F32)
         return total.astype(BF16)
 
-    with jax.named_scope("rows_first"):
-        gather_step(0, 1)
-        rings_a[1].start()
-        rings_b[1].start()
+    with jax.named_scope("rows"):
+        gather_step(1)
+        ring_w.start()
         for load in loads[3:]:
             load.wait()
         for swap in (swap_att, swap_aux, swap_part, swap_stream):
             swap.wait_send()
-    with jax.named_scope("rows_rest"):
-        gather_step(0, 2)
-        gather_step(1, 1)
-        gather_step(0, 3)
-        gather_step(1, 2)
-        gather_step(0, 4)
+        gather_step(2)
+        ring_w.step(1)
+        gather_step(3)
+        ring_w.step(2)
+        gather_step(4)
         activate(0)
-        gather_step(1, 3)
         lower(h, 0, True)
-        for pair in first_swaps:
-            for swap in pair:
-                swap.wait_send()
-        gather_step(1, 4)
+        ring_w.step(3)
     with jax.named_scope("hidden_units"):
         hidden_step(0, 1)
+        for swap in (swap_a, swap_b, swap_w):
+            swap.wait_send()
+        ring_w.step(4)
         activate(1)
         hidden_step(0, 2)
         lower(h, 1, True)
-        hidden_step(1, 1)
         mixing = mix()
         hidden_step(0, 3)
-        hidden_step(1, 2)
-        for ring in rings_a + rings_b:
-            ring.wait_send()
+        hidden_step(1, 1)
         hidden_step(0, 4)
         hand_over(0)
+        for ring in (ring_a, ring_b, ring_w):
+            ring.wait_send()
+        hidden_step(1, 2)
         hidden_step(1, 3)
+        first_rows = collect(0)
         hidden_step(1, 4)
         hand_over(1)
         for ring in rings_h:
             ring.wait_send()
 
     with jax.named_scope("collect"):
-        expert_rows = jnp.concatenate([collect(m) for m in range(micro)], axis=0)
+        expert_rows = jnp.concatenate([first_rows, collect(1)], axis=0)
         back_send[...] = dot(sorted_rows[...], expert_rows).reshape(n, slots, width)
 
     def back(to, at):
@@ -580,11 +556,14 @@
         pltpu.VMEM((n, tokens, width), BF16),
         pltpu.VMEM((n, tokens, width), BF16),
         pltpu.VMEM((n, tokens, width), BF16),
-        pltpu.VMEM((micro, n, n // 2 * SLOTS, width), BF16),
-        pltpu.VMEM((micro, n, n // 2 * SLOTS, width), BF16),
-        pltpu.VMEM((n, micro, block_rows, features // 2), BF16),
-        pltpu.VMEM((n, micro, block_rows, features // 2), BF16),
-        pltpu.VMEM((micro, n // 2 * SLOTS, n // 2 * tokens), BF16),
+        pltpu.VMEM((n, n // 2 * SLOTS, width), BF16),
+        pltpu.VMEM((n, n // 2 * SLOTS, width), BF16),
+        pltpu.VMEM((n, n * SLOTS, width), BF16),
+        pltpu.VMEM((n, block_rows, features // 2), BF16),
+        pltpu.VMEM((n, block_rows, features // 2), BF16),
+        pltpu.VMEM((n, block_rows, features), BF16),
+        pltpu.VMEM((n // 2 * SLOTS, n // 2 * tokens), BF16),
+        pltpu.VMEM((n * SLOTS, n * tokens), BF16),
         pltpu.VMEM((n * n // 2 * SLOTS, n * n // 2 * SLOTS), BF16),
         pltpu.VMEM((all_rows, all_rows), BF16),
         pltpu.VMEM((micro * block_rows, micro * block_rows), BF16),
@@ -595,8 +574,8 @@
         pltpu.VMEM((n, slots, width), F32),
         pltpu.VMEM((n, slots, width), F32),
         pltpu.SemaphoreType.DMA((6,)),
-        pltpu.SemaphoreType.DMA((10, 2)),
-        pltpu.SemaphoreType.DMA((3 * micro, 4, n // 2)),
+        pltpu.SemaphoreType.DMA((9, 2)),
+        pltpu.SemaphoreType.DMA((3 + micro, 4, n // 2)),
         pltpu.SemaphoreType.DMA((2,)),
     ]
     return pl.pallas_call(

time: 94.8 us -> 99.5 us (1.050)
  Pallas kernels: 93.1 us -> 97.9 us
    pallas_call x1, Pallas kernels: 93.1 us -> 97.9 us  [per_device(): pl.pallas_call(functools.partial(layer, n), out_shape=jax.ShapeDtypeStruc...]
where the time goes in v6:
time: 99.5 us; the launch traced here: 99.3 us
  Pallas kernels  97.9 us (98%)
  local copies, waits for them, and re-layouts  1.31 us (1%)
    pallas_call x1, Pallas kernels, per_device(): pl.pallas_call(functools.partial(layer, n), out_shape=jax.ShapeDtypeStruc...  97.9 us

profile of v6, /device:TPU:1, one launch (start us, length us, event | category | flops | bytes accessed | tf_op | source)
XLA Modules:
  0.0 99.3 jit_solution(1666125967417071826)
XLA Ops:
  0.0 97.9 %shard_map.118 = bf16[2,8,384]{2,1,0:T(8,128)(2,1)} custom-call(bf16[2,8,384]{2,1,0:T(8,128)(2,1)} %query_ref.1, bf16[2,8,32,128]{3,2,1,0:T(8,128)(2,1)} %keys_hbm.1, bf16[2,8,32,128]{3,2,1,0:T(8,128)(2,1)} %values_hbm.1, s32[2,8]{1,0:T(2,128)} %lengths_ref.1, bf16[384,384]{1,0:T(8,128)(2,1)} %proj_hbm.1, bf16[2,8,384]{2,1,0:T(8,128)(2,1)} %residual_ref.1, ...), custom_call_target="tpu_custom_call" | custom-call | tf_op jit(solution)/shard_map/pallas_call | solution.py:581
  97.9 1.3 %copy.14 = bf16[2,8,384]{2,1,0:T(8,128)(2,1)} copy(bf16[2,8,384]{2,1,0:T(8,128)(2,1)} %shard_map.118) | data formatting | bytes 24576

commit v7 on v5

--- a/solution.py
+++ b/solution.py
@@ -424,8 +424,10 @@
         rings_a[m].step(k)
         rings_b[m].step(k)
 
-    def hidden_step(m, k):
+    def hidden_step(m, k, first=False):
         rings_h[m].step(k)
+        if first:
+            lower(h, m, True)
         for b in rings_h[m].blocks(k):
             lower(b, m)
 
@@ -452,41 +454,38 @@
             total += down_recv[m, lax.rem(r + d, n)].astype(F32)
         return total.astype(BF16)
 
-    with jax.named_scope("rows_first"):
-        gather_step(0, 1)
+    with jax.named_scope("rows"):
         rings_a[1].start()
         rings_b[1].start()
+        gather_step(0, 1)
         for load in loads[3:]:
             load.wait()
+        gather_step(1, 1)
         for swap in (swap_att, swap_aux, swap_part, swap_stream):
             swap.wait_send()
-    with jax.named_scope("rows_rest"):
         gather_step(0, 2)
-        gather_step(1, 1)
+        gather_step(1, 2)
         gather_step(0, 3)
-        gather_step(1, 2)
+        gather_step(1, 3)
         gather_step(0, 4)
         activate(0)
-        gather_step(1, 3)
-        lower(h, 0, True)
+        gather_step(1, 4)
+    with jax.named_scope("hidden_units"):
+        activate(1)
+        hidden_step(0, 1, True)
+        hidden_step(1, 1, True)
         for pair in first_swaps:
             for swap in pair:
                 swap.wait_send()
-        gather_step(1, 4)
-    with jax.named_scope("hidden_units"):
-        hidden_step(0, 1)
-        activate(1)
         hidden_step(0, 2)
-        lower(h, 1, True)
-        hidden_step(1, 1)
         mixing = mix()
-        hidden_step(0, 3)
         hidden_step(1, 2)
         for ring in rings_a + rings_b:
             ring.wait_send()
+        hidden_step(0, 3)
+        hidden_step(1, 3)
         hidden_step(0, 4)
         hand_over(0)
-        hidden_step(1, 3)
         hidden_step(1, 4)
         hand_over(1)
         for ring in rings_h:

time: 94.8 us -> 89.8 us (0.947)
  Pallas kernels: 93.1 us -> 88.2 us
    pallas_call x1, Pallas kernels: 93.1 us -> 88.2 us  [per_device(): pl.pallas_call(functools.partial(layer, n), out_shape=jax.ShapeDtypeStruc...]
where the time goes in v7:
time: 89.8 us; the launch traced here: 89.5 us
  Pallas kernels  88.2 us (98%)
  local copies, waits for them, and re-layouts  1.31 us (1%)
    pallas_call x1, Pallas kernels, per_device(): pl.pallas_call(functools.partial(layer, n), out_shape=jax.ShapeDtypeStruc...  88.2 us

profile of v7, /device:TPU:1, one launch (start us, length us, event | category | flops | bytes accessed | tf_op | source)
XLA Modules:
  0.0 89.5 jit_solution(2688070652182385327)
XLA Ops:
  0.0 88.2 %shard_map.118 = bf16[2,8,384]{2,1,0:T(8,128)(2,1)} custom-call(bf16[2,8,384]{2,1,0:T(8,128)(2,1)} %query_ref.1, bf16[2,8,32,128]{3,2,1,0:T(8,128)(2,1)} %keys_hbm.1, bf16[2,8,32,128]{3,2,1,0:T(8,128)(2,1)} %values_hbm.1, s32[2,8]{1,0:T(2,128)} %lengths_ref.1, bf16[384,384]{1,0:T(8,128)(2,1)} %proj_hbm.1, bf16[2,8,384]{2,1,0:T(8,128)(2,1)} %residual_ref.1, ...), custom_call_target="tpu_custom_call" | custom-call | tf_op jit(solution)/shard_map/pallas_call | solution.py:601
  88.2 1.3 %copy.14 = bf16[2,8,384]{2,1,0:T(8,128)(2,1)} copy(bf16[2,8,384]{2,1,0:T(8,128)(2,1)} %shard_map.118) | data formatting | bytes 24576

commit v8 on v7

--- a/solution.py
+++ b/solution.py
@@ -389,7 +389,9 @@
         settle_b(0)
         rings_b[0].start()
         settle_a(1)
+        rings_a[1].start()
         settle_b(1)
+        rings_b[1].start()
 
     def mix():
         logits = jnp.zeros((tokens, 2 * n), F32)
@@ -455,14 +457,10 @@
         return total.astype(BF16)
 
     with jax.named_scope("rows"):
-        rings_a[1].start()
-        rings_b[1].start()
         gather_step(0, 1)
         for load in loads[3:]:
             load.wait()
         gather_step(1, 1)
-        for swap in (swap_att, swap_aux, swap_part, swap_stream):
-            swap.wait_send()
         gather_step(0, 2)
         gather_step(1, 2)
         gather_step(0, 3)
@@ -474,21 +472,18 @@
         activate(1)
         hidden_step(0, 1, True)
         hidden_step(1, 1, True)
-        for pair in first_swaps:
-            for swap in pair:
-                swap.wait_send()
         hidden_step(0, 2)
-        mixing = mix()
         hidden_step(1, 2)
-        for ring in rings_a + rings_b:
-            ring.wait_send()
         hidden_step(0, 3)
         hidden_step(1, 3)
         hidden_step(0, 4)
         hand_over(0)
         hidden_step(1, 4)
         hand_over(1)
-        for ring in rings_h:
+        mixing = mix()
+        for swap in (swap_att, swap_aux, swap_part, swap_stream, *first_swaps[0], *first_swaps[1]):
+            swap.wait_send()
+        for ring in rings_a + rings_b + rings_h:
             ring.wait_send()
 
     with jax.named_scope("collect"):

time: 89.8 us -> 89.8 us (level)
  no operation moved by 1% of the time
where the time goes in v8:
time: 89.8 us; the launch traced here: 89.5 us
  Pallas kernels  88.2 us (98%)
  local copies, waits for them, and re-layouts  1.31 us (1%)
    pallas_call x1, Pallas kernels, per_device(): pl.pallas_call(functools.partial(layer, n), out_shape=jax.ShapeDtypeStruc...  88.2 us

profile of v8, /device:TPU:1, one launch (start us, length us, event | category | flops | bytes accessed | tf_op | source)
XLA Modules:
  0.0 89.5 jit_solution(12454378946325142265)
XLA Ops:
  0.0 88.2 %shard_map.118 = bf16[2,8,384]{2,1,0:T(8,128)(2,1)} custom-call(bf16[2,8,384]{2,1,0:T(8,128)(2,1)} %query_ref.1, bf16[2,8,32,128]{3,2,1,0:T(8,128)(2,1)} %keys_hbm.1, bf16[2,8,32,128]{3,2,1,0:T(8,128)(2,1)} %values_hbm.1, s32[2,8]{1,0:T(2,128)} %lengths_ref.1, bf16[384,384]{1,0:T(8,128)(2,1)} %proj_hbm.1, bf16[2,8,384]{2,1,0:T(8,128)(2,1)} %residual_ref.1, ...), custom_call_target="tpu_custom_call" | custom-call | tf_op jit(solution)/shard_map/pallas_call | solution.py:596
  88.2 1.3 %copy.14 = bf16[2,8,384]{2,1,0:T(8,128)(2,1)} copy(bf16[2,8,384]{2,1,0:T(8,128)(2,1)} %shard_map.118) | data formatting | bytes 24576
